TPU v7x, 32 devices: a whole 2x2x4 slice. The times are simulated.
32 devices in a mesh: dp: 4 (over z), expert: 2 (over y), tensor: 4 (over x, core).
Axes of the slice: x: 2, y: 2, z: 4, core: 2. Of those that a mesh axis runs over, the one named last changes fastest.
Arguments:
- tokens: bfloat16 [2, 4096, 768], P(None, ('dp', 'expert', 'tensor')), may hold values from -6 to 6
- cotangent: bfloat16 [2, 4096, 768], P(None, ('dp', 'expert', 'tensor')), may hold values from -6 to 6
- row_order: int32 [2, 8, 512], P(None, ('dp', 'expert')), may hold values from 0 to 511, each once within a row
- lengths: int32 [2, 8, 3], P(None, ('dp', 'expert')), may hold values from 1 to 341, 512 in all within a row
- routes: int32 [2, 2, 4096, 2], P(None, None, ('dp', 'expert', 'tensor')), may hold values from 0 to 5, all different within a row; in each aligned block of 128 rows (0 to 127, 128 to 255, ..., all dimensions but the last counted through in order) at most 48 rows name the same one
- norm_gains: float32 [2, 2, 768], replicated, may hold values from 0.25 to 1.75
- w_qkv: bfloat16 [2, 3, 768, 768], P(None, None, None, 'tensor'), may hold values from -0.21875 to 0.21875
- w_out: bfloat16 [2, 768, 768], P(None, 'tensor'), may hold values from -3 to 3
- w_gate_up: bfloat16 [2, 2, 2, 768, 2048], P(None, 'expert', None, None, 'tensor'), may hold values from -0.21875 to 0.21875
- w_down: bfloat16 [2, 2, 2048, 768], P(None, 'expert', 'tensor'), may hold values from -0.25 to 0.25
- w_router: float32 [2, 768, 6], replicated, may hold values from -0.15 to 0.15
- const_proj: float32 [2, 768, 4], replicated, may hold values from -0.2 to 0.2
- const_vec: float32 [2, 2, 768], replicated, may hold values from -6 to 6
Outputs:
- block_out: bfloat16 [2, 4096, 768], P(None, ('dp', 'expert', 'tensor'))
- grad_tokens: float32 [2, 4096, 768], P(None, ('dp', 'expert', 'tensor'))
- grad_gains: float32 [2, 768], replicated
- grad_moe_gains: float32 [2, 768], replicated
- grad_qkv: float32 [2, 3, 768, 768], P(None, None, ('dp', 'expert'), 'tensor')
- grad_out_proj: float32 [2, 768, 768], P(None, 'tensor', ('dp', 'expert'))
- grad_gate_up: float32 [2, 2, 2, 768, 2048], P(None, 'expert', None, 'dp', 'tensor')
- grad_down: float32 [2, 2, 2048, 768], P(None, 'expert', 'tensor', 'dp')
- grad_router: float32 [2, 768, 6], replicated
- grad_const_proj: float32 [2, 768, 4], replicated
- grad_const_vec: float32 [2, 2, 768], replicated
Inputs may be any that keep to these rules, and one draw needn't show every extreme that they name: Each pack's row_order holds every position of the pack once. Each pack has 3 documents whose lengths sum to 512; the longest has exactly 341 tokens. A token's two routes differ. Routes below 2 are feed-forward experts, 2 is the zero expert, 3 the copy expert, 4 and 5 the constant experts. Among the rows of one device in one layer and micro-batch no route is named by more than 48 rows, a bound that some block reaches.
All inputs are finite; a program needn't handle non-finite values.
Results may differ from a plain program's by a relative error of at most 0.03.
The roundings to bfloat16 on the way count: a program that leaves them out, or rounds other values in their place, can miss the bound.
Values may be sent and summed in bfloat16 or wider, within the bound.
No kernel may reach another device: no remote copies, remote signals or barrier semaphores. Data moves between devices by JAX's collectives and lax.ppermute only.
A program may use at most 192 MiB of HBM per device.

v0:
```python
import math

import jax
import jax.numpy as jnp
from jax import lax
from jax.sharding import PartitionSpec as P

HDIM = 64


epsilon = 1e-06
score_scale = 0.125
masked_value = -1e30
highest = lax.Precision.HIGHEST


def cut_along(shard, dim, length):
    before, after = (shard.shape[:dim], shard.shape[dim + 1 :])
    return jnp.moveaxis(shard.reshape(*before, length, -1, *after), dim, 0)


def sum_at_owner(shard, axis, dim):
    pieces = cut_along(shard, dim, lax.axis_size(axis))
    arrived = lax.all_to_all(pieces, axis, split_axis=0, concat_axis=0, tiled=True)
    return arrived.astype(jnp.float32).sum(axis=0)


def positions(order_row, lengths_row):
    starts = jnp.cumsum(lengths_row, dtype=jnp.int32) - lengths_row
    reached = order_row[:, None] >= starts[None, :]
    segment = jnp.sum(reached.astype(jnp.int32), axis=1, dtype=jnp.int32)
    offset = jnp.max(jnp.where(reached, starts[None, :], 0), axis=1)
    return (segment, order_row - offset)


def rope_tables(relative):
    half_dim = HDIM // 2
    frequency = jnp.exp(-math.log(10000.0) * jnp.arange(half_dim, dtype=jnp.float32) / half_dim)
    angles = relative.astype(jnp.float32)[:, None] * frequency[None, :]
    return (jnp.cos(angles), jnp.sin(angles))


def rotate(values, cosine, sine_table):
    half_dim = values.shape[-1] // 2
    first_half = values[..., :half_dim]
    second_half = values[..., half_dim:]
    cos_part = cosine[:, None, :]
    sin_part = sine_table[:, None, :]
    return jnp.concatenate(
        [
            first_half * cos_part - second_half * sin_part,
            second_half * cos_part + first_half * sin_part,
        ],
        axis=-1,
    )


def row_norm(stream, gain):
    scale_rows = lax.rsqrt(jnp.mean(stream * stream, axis=-1, keepdims=True) + epsilon)
    unit_rows = stream * scale_rows
    return (unit_rows * gain, unit_rows, scale_rows)


def norm_back(grad_norm, unit_rows, scale_rows, gain):
    grad_unit = grad_norm * gain
    grad_stream = scale_rows * (
        grad_unit - unit_rows * jnp.mean(grad_unit * unit_rows, axis=-1, keepdims=True)
    )
    return (grad_stream, jnp.sum(grad_norm * unit_rows, axis=0))


def spread_rows(rows_low):
    return lax.all_gather(rows_low, "tensor", axis=0, tiled=True)


def sum_rows(left_rows, product):
    return lax.psum_scatter(
        product(left_rows).astype(jnp.bfloat16), "tensor", scatter_dimension=0, tiled=True
    ).astype(jnp.float32)


def send_rows(buffer):
    experts_n = buffer.shape[0]
    model_width = buffer.shape[2]
    tensor_n = lax.axis_size("tensor")
    copied = jnp.broadcast_to(buffer[:, None], (experts_n, tensor_n) + buffer.shape[1:]).reshape(
        (experts_n * tensor_n,) + buffer.shape[1:]
    )
    copies = lax.all_to_all(copied, ("expert", "tensor"), split_axis=0, concat_axis=0, tiled=True)
    return copies.reshape(-1, model_width)


def return_rows(partial_value, capacity):
    experts_n = lax.axis_size("expert")
    tensor_n = lax.axis_size("tensor")
    model_width = partial_value.shape[1]
    source_slabs = partial_value.reshape(experts_n * tensor_n, capacity, model_width)
    arrived = lax.all_to_all(
        source_slabs.astype(jnp.bfloat16),
        ("expert", "tensor"),
        split_axis=0,
        concat_axis=0,
        tiled=True,
    ).astype(source_slabs.dtype)
    gathered_back = jnp.sum(arrived.reshape(experts_n, tensor_n, capacity, model_width), axis=1)
    return gathered_back.reshape(experts_n * capacity, model_width)


def slot_tables(routes_now, experts_n, capacity):
    pair_routes = routes_now.reshape(-1)
    pair_count = pair_routes.shape[0]
    member = (pair_routes[:, None] == jnp.arange(experts_n, dtype=jnp.int32)[None, :]).astype(
        jnp.int32
    )
    earlier = jnp.cumsum(member, axis=0, dtype=jnp.int32) - member
    rank_in = jnp.sum(earlier * member, axis=1, dtype=jnp.int32)
    slot_index = jnp.where(
        pair_routes < experts_n, pair_routes * capacity + rank_in, experts_n * capacity
    )
    owner_pair = (
        jnp.full((experts_n * capacity + 1,), pair_count, jnp.int32)
        .at[slot_index]
        .set(jnp.arange(pair_count, dtype=jnp.int32))
    )
    return (slot_index, owner_pair[: experts_n * capacity])


def attend_forward(h_full, qkv_layer, cosine, sine_table, allowed):
    seq_len = h_full.shape[0]
    local_width = qkv_layer.shape[2]
    heads_local = local_width // HDIM
    projected = jnp.einsum("sd,cdf->csf", h_full, qkv_layer, preferred_element_type=jnp.float32)
    shaped = projected.reshape(3, seq_len, heads_local, HDIM)
    queries = rotate(shaped[0], cosine, sine_table).astype(jnp.bfloat16)
    key_rows = rotate(shaped[1], cosine, sine_table).astype(jnp.bfloat16)
    values = shaped[2].astype(jnp.bfloat16)
    scores = (
        jnp.einsum("qhd,khd->hqk", queries, key_rows, preferred_element_type=jnp.float32)
        * score_scale
    )
    scores = jnp.where(allowed[None, 0:seq_len], scores, masked_value)
    row_peak = jnp.max(scores, axis=-1, keepdims=True)
    exponent = jnp.exp(scores - row_peak)
    row_total = jnp.sum(exponent, axis=-1, keepdims=True)
    attention = (exponent / row_total).astype(jnp.bfloat16)
    outputs = jnp.einsum("hqk,khd->qhd", attention, values, preferred_element_type=jnp.float32)
    log_totals = [row_peak + jnp.log(row_total)]
    mixed = outputs.reshape(seq_len, local_width).astype(jnp.bfloat16)
    return (mixed, (queries, key_rows, values, log_totals))


def attend_backward(grad_mixed, attn_kept, allowed, cosine, sine_table):
    queries, key_rows, values, log_totals = attn_kept
    seq_len = queries.shape[0]
    heads_local = queries.shape[1]
    local_width = heads_local * HDIM
    grad_heads = grad_mixed.reshape(seq_len, heads_local, HDIM)
    grad_query_parts = []
    grad_keys = jnp.zeros(key_rows.shape, jnp.float32)
    grad_values = jnp.zeros(values.shape, jnp.float32)
    for block_index, block_start in enumerate(range(0, seq_len, seq_len)):
        block_end = block_start + seq_len
        scores = (
            jnp.einsum("qhd,khd->hqk", queries, key_rows, preferred_element_type=jnp.float32)
            * score_scale
        )
        scores = jnp.where(allowed[None, block_start:block_end], scores, masked_value)
        attention = jnp.exp(scores - log_totals[block_index])
        grad_attention = jnp.einsum(
            "qhd,khd->hqk", grad_heads, values, preferred_element_type=jnp.float32
        )
        grad_values = jnp.einsum(
            "hqk,qhd->khd",
            attention.astype(jnp.bfloat16),
            grad_heads,
            preferred_element_type=jnp.float32,
        )
        grad_scores = (
            attention
            * (grad_attention - jnp.sum(attention * grad_attention, axis=-1, keepdims=True))
        ).astype(jnp.bfloat16)
        grad_query_parts.append(
            jnp.einsum("hqk,khd->qhd", grad_scores, key_rows, preferred_element_type=jnp.float32)
            * score_scale
        )
        grad_keys = (
            jnp.einsum("hqk,qhd->khd", grad_scores, queries, preferred_element_type=jnp.float32)
            * score_scale
        )
    grad_queries = grad_query_parts[0]
    grad_query_raw = rotate(grad_queries, cosine, -sine_table).reshape(seq_len, local_width)
    grad_key_raw = rotate(grad_keys, cosine, -sine_table).reshape(seq_len, local_width)
    return jnp.stack(
        [grad_query_raw, grad_key_raw, grad_values.reshape(seq_len, local_width)], axis=1
    ).astype(jnp.bfloat16)


def layer_forward(stream, previous, routes_now, weights, tables):
    (
        gains_layer,
        qkv_layer,
        out_layer,
        gate_up_layer,
        down_layer,
        router_layer,
        proj_layer,
        vec_layer,
    ) = weights
    cosine, sine_table, allowed = tables
    experts_n = lax.axis_size("expert")
    rows_here = stream.shape[0]
    model_width = stream.shape[1]
    capacity = 9 * rows_here // (4 * (experts_n + 4))
    h_attn, unit_attn, scale_attn = row_norm(stream, gains_layer[0])
    h_full = spread_rows(h_attn.astype(jnp.bfloat16))
    mixed, attn_kept = attend_forward(h_full, qkv_layer, cosine, sine_table, allowed)

    def out_product(block_part):
        return jnp.dot(block_part, out_layer, preferred_element_type=jnp.float32)

    attn_term = sum_rows(mixed, out_product)
    stream_mid = stream + attn_term
    h_moe, unit_moe, scale_moe = row_norm(stream_mid, gains_layer[1])
    h_moe_low16 = h_moe.astype(jnp.bfloat16)
    h_moe_low = h_moe_low16.astype(jnp.float32)
    logits = jnp.dot(h_moe_low, router_layer, precision=highest) + previous
    chosen = (
        routes_now[:, :, None] == jnp.arange(experts_n + 4, dtype=jnp.int32)[None, None, :]
    ).astype(jnp.float32)
    picked = jnp.sum(chosen * logits[:, None, :], axis=-1)
    gate_exp = jnp.exp(picked - jnp.max(picked, axis=-1, keepdims=True))
    gate_weights = gate_exp / jnp.sum(gate_exp, axis=-1, keepdims=True)
    const_logits = jnp.dot(h_moe_low, proj_layer, precision=highest).reshape(rows_here, 2, 2)
    const_exp = jnp.exp(const_logits - jnp.max(const_logits, axis=-1, keepdims=True))
    mixing = const_exp / jnp.sum(const_exp, axis=-1, keepdims=True)
    const_out = (
        mixing[:, :, 0:1] * h_moe_low[:, None, :] + mixing[:, :, 1:2] * vec_layer[None, :, :]
    )
    slot_index, owner_pair = slot_tables(routes_now, experts_n, capacity)
    padded_rows = jnp.concatenate([h_moe_low16, jnp.zeros((1, model_width), jnp.bfloat16)], axis=0)
    buffer = jnp.take(padded_rows, owner_pair // 2, axis=0).reshape(
        experts_n, capacity, model_width
    )
    owner_rows = send_rows(buffer)
    gate_up_pre = jnp.einsum(
        "rd,cdf->crf", owner_rows, gate_up_layer, preferred_element_type=jnp.float32
    )
    hidden = (jax.nn.silu(gate_up_pre[0]) * gate_up_pre[1]).astype(jnp.bfloat16)
    partial_value = jnp.dot(hidden, down_layer, preferred_element_type=jnp.float32)
    expert_out = return_rows(partial_value, capacity)
    padded_out = jnp.concatenate([expert_out, jnp.zeros((1, model_width), jnp.float32)], axis=0)
    pair_out = jnp.take(padded_out, slot_index, axis=0).reshape(rows_here, 2, model_width)
    is_copy = (routes_now == experts_n + 1).astype(jnp.float32)[:, :, None]
    const_pick = (
        routes_now[:, :, None] == experts_n + 2 + jnp.arange(2, dtype=jnp.int32)[None, None, :]
    ).astype(jnp.float32)
    route_value = (
        pair_out
        + is_copy * h_moe_low[:, None, :]
        + jnp.einsum("qkj,qjd->qkd", const_pick, const_out, precision=highest)
    )
    stream_out = stream_mid + jnp.sum(gate_weights[:, :, None] * route_value, axis=1)
    kept_state = (
        unit_attn,
        scale_attn,
        h_full,
        attn_kept,
        mixed,
        unit_moe,
        scale_moe,
        h_moe_low,
        gate_weights,
        route_value,
        mixing,
        const_pick,
        is_copy,
        slot_index,
        owner_pair,
        owner_rows,
        gate_up_pre,
        hidden,
    )
    return (stream_out, logits, kept_state)


def layer_backward(grad_out, grad_next_logits, routes_now, weights, kept_state, tables):
    (
        gains_layer,
        qkv_layer,
        out_layer,
        gate_up_layer,
        down_layer,
        router_layer,
        proj_layer,
        vec_layer,
    ) = weights
    cosine, sine_table, allowed = tables
    (
        unit_attn,
        scale_attn,
        h_full,
        attn_kept,
        mixed,
        unit_moe,
        scale_moe,
        h_moe_low,
        gate_weights,
        route_value,
        mixing,
        const_pick,
        is_copy,
        slot_index,
        owner_pair,
        owner_rows,
        gate_up_pre,
        hidden,
    ) = kept_state
    experts_n = lax.axis_size("expert")
    rows_here = grad_out.shape[0]
    model_width = grad_out.shape[1]
    capacity = owner_pair.shape[0] // experts_n
    grad_choice = jnp.sum(grad_out[:, None, :] * route_value, axis=-1)
    grad_picked = gate_weights * (
        grad_choice - jnp.sum(gate_weights * grad_choice, axis=-1, keepdims=True)
    )
    chosen = (
        routes_now[:, :, None] == jnp.arange(experts_n + 4, dtype=jnp.int32)[None, None, :]
    ).astype(jnp.float32)
    grad_logits = jnp.sum(chosen * grad_picked[:, :, None], axis=1) + grad_next_logits
    grad_router = jnp.dot(h_moe_low.T, grad_logits, precision=highest)
    grad_h = jnp.dot(grad_logits, router_layer.T, precision=highest)
    weighted = gate_weights[:, :, None] * grad_out[:, None, :]
    grad_h = grad_h + jnp.sum(is_copy * weighted, axis=1)
    grad_const = jnp.einsum("qkj,qkd->qjd", const_pick, weighted, precision=highest)
    grad_mix = jnp.stack(
        [
            jnp.sum(grad_const * h_moe_low[:, None, :], axis=-1),
            jnp.sum(grad_const * vec_layer[None, :, :], axis=-1),
        ],
        axis=-1,
    )
    grad_const_logits = (
        mixing * (grad_mix - jnp.sum(mixing * grad_mix, axis=-1, keepdims=True))
    ).reshape(rows_here, 4)
    grad_vec = jnp.sum(mixing[:, :, 1:2] * grad_const, axis=0)
    grad_h = (
        grad_h
        + jnp.sum(mixing[:, :, 0:1] * grad_const, axis=1)
        + jnp.dot(grad_const_logits, proj_layer.T, precision=highest)
    )
    grad_proj = jnp.dot(h_moe_low.T, grad_const_logits, precision=highest)
    routed = (routes_now < experts_n)[:, :, None]
    pair_grad = (
        jnp.where(routed, weighted, 0.0).astype(jnp.bfloat16).reshape(2 * rows_here, model_width)
    )
    padded_grad = jnp.concatenate([pair_grad, jnp.zeros((1, model_width), jnp.bfloat16)], axis=0)
    grad_buffer = jnp.take(padded_grad, owner_pair, axis=0).reshape(
        experts_n, capacity, model_width
    )
    grad_rows = send_rows(grad_buffer)
    grad_hidden = jnp.dot(grad_rows, down_layer.T, preferred_element_type=jnp.float32)
    grad_down = jnp.dot(hidden.T, grad_rows, preferred_element_type=jnp.float32)
    gate_pre = gate_up_pre[0]
    up_pre = gate_up_pre[1]
    gate_sigmoid = jax.nn.sigmoid(gate_pre)
    grad_gate = (
        grad_hidden * up_pre * gate_sigmoid * (1.0 + gate_pre * (1.0 - gate_sigmoid))
    ).astype(jnp.bfloat16)
    grad_up = (grad_hidden * gate_pre * gate_sigmoid).astype(jnp.bfloat16)
    grad_both = jnp.stack([grad_gate, grad_up])
    grad_gate_up = jnp.einsum(
        "rd,crf->cdf", owner_rows, grad_both, preferred_element_type=jnp.float32
    )
    grad_rows_in = jnp.einsum(
        "crf,cdf->rd", grad_both, gate_up_layer, preferred_element_type=jnp.float32
    )
    returned = return_rows(grad_rows_in, capacity)
    padded_back = jnp.concatenate([returned, jnp.zeros((1, model_width), jnp.float32)], axis=0)
    grad_h = grad_h + jnp.sum(
        jnp.take(padded_back, slot_index, axis=0).reshape(rows_here, 2, model_width), axis=1
    )
    grad_mid, grad_gain_moe = norm_back(grad_h, unit_moe, scale_moe, gains_layer[1])
    grad_mid = grad_mid + grad_out
    grad_attn_full = spread_rows(grad_mid.astype(jnp.bfloat16))
    grad_mixed = jnp.dot(grad_attn_full, out_layer.T, preferred_element_type=jnp.float32).astype(
        jnp.bfloat16
    )
    grad_out_layer = jnp.dot(mixed.T, grad_attn_full, preferred_element_type=jnp.float32)
    grad_qkv_rows = attend_backward(grad_mixed, attn_kept, allowed, cosine, sine_table)
    grad_qkv_layer = jnp.einsum(
        "sd,scf->cdf", h_full, grad_qkv_rows, preferred_element_type=jnp.float32
    )

    def qkv_product(block_part):
        return jnp.einsum("scf,cdf->sd", block_part, qkv_layer, preferred_element_type=jnp.float32)

    grad_h_attn = sum_rows(grad_qkv_rows, qkv_product)
    grad_stream, grad_gain_attn = norm_back(grad_h_attn, unit_attn, scale_attn, gains_layer[0])
    grad_stream = grad_stream + grad_mid
    layer_grads = (
        jnp.stack([grad_gain_attn, grad_gain_moe]),
        grad_qkv_layer,
        grad_out_layer,
        grad_gate_up,
        grad_down,
        grad_router,
        grad_proj,
        grad_vec,
    )
    return (grad_stream, grad_logits, layer_grads)


def local(
    tokens,
    cotangent,
    row_order,
    lengths,
    routes,
    norm_gains,
    w_qkv,
    w_out,
    w_gate_up,
    w_down,
    w_router,
    const_proj,
    const_vec,
):
    layer_count = w_qkv.shape[0]
    micro_count = tokens.shape[0]
    route_count = w_router.shape[2]
    outputs = []
    grad_inputs = []
    totals = None
    for micro_index in range(micro_count):
        order_now = row_order[micro_index, 0]
        segment, relative = positions(order_now, lengths[micro_index, 0])
        allowed = (segment[:, None] == segment[None, :]) & (
            order_now[None, :] <= order_now[:, None]
        )
        cosine, sine_table = rope_tables(relative)
        tables = (cosine, sine_table, allowed)
        stream = tokens[micro_index].astype(jnp.float32)
        previous = jnp.zeros((stream.shape[0], route_count), jnp.float32)
        stash = []
        for layer_index in range(layer_count):
            weights = (
                norm_gains[layer_index],
                w_qkv[layer_index],
                w_out[layer_index],
                w_gate_up[layer_index, 0],
                w_down[layer_index, 0],
                w_router[layer_index],
                const_proj[layer_index],
                const_vec[layer_index],
            )
            stream, previous, kept_state = layer_forward(
                stream, previous, routes[layer_index, micro_index], weights, tables
            )
            stash.append(kept_state)
        outputs.append(stream.astype(jnp.bfloat16))
        grad_stream = cotangent[micro_index].astype(jnp.float32)
        grad_logits = jnp.zeros_like(previous)
        micro_grads = [None] * layer_count
        for layer_index in reversed(range(layer_count)):
            weights = (
                norm_gains[layer_index],
                w_qkv[layer_index],
                w_out[layer_index],
                w_gate_up[layer_index, 0],
                w_down[layer_index, 0],
                w_router[layer_index],
                const_proj[layer_index],
                const_vec[layer_index],
            )
            grad_stream, grad_logits, layer_grads = layer_backward(
                grad_stream,
                grad_logits,
                routes[layer_index, micro_index],
                weights,
                stash[layer_index],
                tables,
            )
            micro_grads[layer_index] = layer_grads
        grad_inputs.append(grad_stream)
        if totals is None:
            totals = micro_grads
        else:
            totals = [
                jax.tree.map(jnp.add, totals[layer_index], micro_grads[layer_index])
                for layer_index in range(layer_count)
            ]
    stacked = [
        jnp.stack([totals[layer_index][member_index] for layer_index in range(layer_count)])
        for member_index in range(8)
    ]
    grad_qkv, grad_out_proj = (
        sum_at_owner(stacked[1].astype(jnp.bfloat16), ("dp", "expert"), 2),
        sum_at_owner(stacked[2].astype(jnp.bfloat16), ("dp", "expert"), 2),
    )
    grad_gate_up, grad_down = (
        lax.psum_scatter(
            stacked[3][:, None].astype(jnp.bfloat16), "dp", scatter_dimension=3, tiled=True
        ).astype(jnp.float32),
        lax.psum_scatter(
            stacked[4][:, None].astype(jnp.bfloat16), "dp", scatter_dimension=3, tiled=True
        ).astype(jnp.float32),
    )
    gain_totals, grad_router, grad_const_proj, grad_const_vec = lax.psum(
        (stacked[0], stacked[5], stacked[6], stacked[7]), ("dp", "expert", "tensor")
    )
    return (
        jnp.stack(outputs),
        jnp.stack(grad_inputs),
        gain_totals[:, 0],
        gain_totals[:, 1],
        grad_qkv,
        grad_out_proj,
        grad_gate_up,
        grad_down,
        grad_router,
        grad_const_proj,
        grad_const_vec,
    )


def solution(mesh):
    return jax.shard_map(
        local,
        mesh=mesh,
        in_specs=(
            P(None, ("dp", "expert", "tensor"), None),
            P(None, ("dp", "expert", "tensor"), None),
            P(None, ("dp", "expert"), None),
            P(None, ("dp", "expert"), None),
            P(None, None, ("dp", "expert", "tensor"), None),
            P(),
            P(None, None, None, "tensor"),
            P(None, "tensor", None),
            P(None, "expert", None, None, "tensor"),
            P(None, "expert", "tensor", None),
            P(),
            P(),
            P(),
        ),
        out_specs=(
            P(None, ("dp", "expert", "tensor"), None),
            P(None, ("dp", "expert", "tensor"), None),
            P(),
            P(),
            P(None, None, ("dp", "expert"), "tensor"),
            P(None, "tensor", ("dp", "expert")),
            P(None, "expert", None, "dp", "tensor"),
            P(None, "expert", "tensor", "dp"),
            P(),
            P(),
            P(),
        ),
        check_vma=False,
    )
```

profile of v0, /device:TPU:0, one launch (start us, length us, event | category | flops | bytes accessed | tf_op | source)
XLA Modules:
  0.0 982.6 jit_solution(1947236151915741714)
XLA Ops:
  10.6 10.0 %all_gather.24 = bf16[512,768]{1,0:T(8,128)(2,1)S(1)} all-gather(bf16[128,768]{1,0:T(8,128)(2,1)S(1)} %get-tuple-element.235), channel_id=1, replica_groups=mesh['dp'=4,'expert'=2,'tensor'=4] {'tensor'}, dimensions={0}, use_global_device_ids=true | all-gather | bytes 983040 | tf_op jit(solution)/shard_map/all_gather | solution.py:73
  28.0 9.2 all_gather.26
  75.5 3.4 reduce-scatter.13.cloned.1.call-done
  87.0 3.5 all-to-all-start
  91.6 9.4 all-to-all-done
  101.9 3.5 all-to-all-start.4
  110.2 5.6 all-to-all-done.4
  115.8 3.5 all-to-all-start.1
  124.1 5.6 all-to-all-done.1
  129.7 4.2 all-to-all-start.5
  139.9 4.5 all-to-all-done.5
  147.4 6.1 multiply_reduce_fusion.27
  153.6 4.8 multiply_reduce_fusion.25
  159.3 7.6 all_gather.27
  169.2 8.9 all_gather.25
  191.9 15.5 %reduce-scatter.11.cloned.1.call-done = bf16[128,768]{1,0:T(8,128)(2,1)} async-done(((bf16[512,768]{1,0:T(8,128)(2,1)}), bf16[128,768]{1,0:T(8,128)(2,1)}) %reduce-scatter.11.cloned.1.call-update) | async-done | bytes 196624 | tf_op jit(solution)/shard_map/reduce_scatter | solution.py:77
  208.5 25.4 %reduce-scatter.15.cloned.1.call-done = bf16[128,768]{1,0:T(8,128)(2,1)} async-done(((bf16[512,768]{1,0:T(8,128)(2,1)}), bf16[128,768]{1,0:T(8,128)(2,1)}) %reduce-scatter.15.cloned.1.call-update) | async-done | bytes 196624 | tf_op jit(solution)/shard_map/reduce_scatter | solution.py:77
  246.2 3.9 all-to-all-start.2
  250.2 2.9 fusion.146
  253.1 8.1 multiply_reduce_fusion.5
  272.6 4.2 all-to-all-start.8
  281.1 6.1 all-to-all-done.8
  288.2 3.5 all-to-all-start.6
  298.5 3.6 all-to-all-done.6
  303.1 3.5 all-to-all-start.12
  309.2 3.3 fusion.55
  312.5 4.5 all-to-all-done.12
  317.0 3.5 all-to-all-start.3
  327.4 3.5 all-to-all-done.3
  330.9 3.8 all-to-all-start.9
  337.3 3.6 fusion.434
  341.1 4.1 all-to-all-done.9
  345.1 4.2 all-to-all-start.7
  355.4 7.4 multiply_reduce_fusion.23
  363.0 4.1 all-to-all-start.13
  374.6 2.9 all-to-all-done.13
  388.3 7.6 multiply_reduce_fusion.15
  397.0 2.9 multiply_reduce_fusion.28
  399.9 7.7 all_gather.28
  414.2 2.8 fusion.85
  417.1 3.5 fusion.45
  425.9 11.7 %reduce-scatter.17.cloned.1.call-done = bf16[128,768]{1,0:T(8,128)(2,1)} async-done(((bf16[512,768]{1,0:T(8,128)(2,1)}), bf16[128,768]{1,0:T(8,128)(2,1)}) %reduce-scatter.17.cloned.1.call-update) | async-done | bytes 196624 | tf_op jit(solution)/shard_map/reduce_scatter | solution.py:77
  441.8 8.3 all_gather.30
  463.7 3.5 all-to-all-start.10
  468.4 3.0 bitcast_convert_fusion.1
  474.1 2.9 fusion.148
  481.8 3.9 all-to-all-start.11
  485.7 2.8 fusion.266
  491.3 7.5 all-to-all-done.11
  506.0 7.8 multiply_reduce_fusion.6
  519.5 3.5 all-to-all-start.14
  523.7 9.7 all-to-all-done.14
  537.9 3.5 all-to-all-start.15
  545.1 6.7 all-to-all-done.15
  561.5 7.8 all_gather.31
  573.9 8.9 all_gather.29
  610.0 26.6 %reduce-scatter.19.cloned.1.call-done = bf16[128,768]{1,0:T(8,128)(2,1)} async-done(((bf16[512,768]{1,0:T(8,128)(2,1)}), bf16[128,768]{1,0:T(8,128)(2,1)}) %reduce-scatter.19.cloned.1.call-update) | async-done | bytes 196624 | tf_op jit(solution)/shard_map/reduce_scatter | solution.py:77
  642.5 5.9 copy.409
  648.4 4.9 copy.410
  656.7 5.8 all-to-all-start.17
  674.8 8.0 all-to-all-done.17
  682.8 3.6 all-to-all-start.16
  694.1 99.0 %all-reduce.23.cloned.1.call-done = (f32[2,2,768]{2,0,1:T(2,128)}, f32[2,768,6]{1,2,0:T(8,128)}, f32[2,768,4]{1,2,0:T(4,128)}, f32[2,2,768]{2,1,0:T(2,128)}) async-done(((f32[2,2,768]{2,0,1:T(2,128)}, f32[2,768,6]{1,2,0:T(8,128)}, f32[2,768,4]{1,2,0:T(4,128)}, f32[2,2,768]{2,1,0:T(2,128)}), (f32[2,2,768]{2,0,1:T(2,128)}, f32[2,768,6]{1,2,0:T(8,128)}, f32[2,768,4]{1,2,0:T(4,128)}, ...) | async-done | bytes 86032 | tf_op jit(solution)/shard_map/psum | solution.py:508
  797.4 171.3 %all-reduce.25.cloned.1.call-done = (bf16[2,1,2,768,512]{4,2,1,0,3:T(2,128)(2,1)}, bf16[2,1,512,768]{2,0,1,3:T(2,128)(2,1)}) async-done(((bf16[2,1,2,768,512]{4,2,1,0,3:T(2,128)(2,1)}, bf16[2,1,512,768]{2,0,1,3:T(2,128)(2,1)}), (bf16[2,1,2,768,512]{4,2,1,0,3:T(2,128)(2,1)}, bf16[2,1,512,768]{2,0,1,3:T(2,128)(2,1)})) %all-reduce.25.cloned.1.call-update) | async-done | bytes 4718608
  (1229 shorter events, 309.3 us)
Async XLA Ops:
  7.2 68.3 %reduce-scatter.9.cloned.1.call-start = ((), (), s32[]{:S(2)}) async-start(), calls=%async_computation.26 | async-start | bytes 983040 | tf_op jit(solution)/shard_map/reduce_scatter | solution.py:77
  9.4 70.8 %copy-start.223 = (f32[768]{0:T(1024)}, f32[768]{0:T(1024)S(1)}, u32[]{:S(2)}) copy-start(f32[768]{0:T(1024)S(1)} %get-tuple-element.120) | copy-start | bytes 9220
  28.0 50.9 %reduce-scatter.13.cloned.1.call-start = ((), (), s32[]{:S(2)}) async-start(), calls=%async_computation.28 | async-start | bytes 983040 | tf_op jit(solution)/shard_map/reduce_scatter | solution.py:77
  41.1 18.9 %copy-start.126 = (bf16[3,64,512]{2,1,0:T(8,128)(2,1)}, bf16[3,64,512]{2,1,0:T(8,128)(2,1)S(1)}, u32[]{:S(2)}) copy-start(bf16[3,64,512]{2,1,0:T(8,128)(2,1)S(1)} %fusion.109) | copy-start | bytes 589828
  41.1 19.6 %copy-start.38 = (bf16[2,128,768]{2,1,0:T(8,128)(2,1)S(1)}, bf16[2,128,768]{2,1,0:T(8,128)(2,1)}, u32[]{:S(2)}) copy-start(bf16[2,128,768]{2,1,0:T(8,128)(2,1)} %param.20) | copy-start | bytes 1179652
  43.1 17.8 %copy-start.270 = (s32[128,2]{0,1:T(2,128)}, s32[128,2]{0,1:T(2,128)S(1)}, u32[]{:S(2)}) copy-start(s32[128,2]{0,1:T(2,128)S(1)} %get-tuple-element.273) | copy-start | bytes 3076
  43.1 19.5 %copy-start.267 = (s32[128,2]{0,1:T(2,128)}, s32[128,2]{0,1:T(2,128)S(1)}, u32[]{:S(2)}) copy-start(s32[128,2]{0,1:T(2,128)S(1)} %get-tuple-element.279) | copy-start | bytes 3076
  43.1 40.9 %copy-start.265 = (s32[128,2]{0,1:T(2,128)}, s32[128,2]{0,1:T(2,128)S(1)}, u32[]{:S(2)}) copy-start(s32[128,2]{0,1:T(2,128)S(1)} %get-tuple-element.274) | copy-start | bytes 3076
  43.1 41.5 %copy-start.263 = (s32[128,2]{0,1:T(2,128)}, s32[128,2]{0,1:T(2,128)S(1)}, u32[]{:S(2)}) copy-start(s32[128,2]{0,1:T(2,128)S(1)} %get-tuple-element.277) | copy-start | bytes 3076
  51.5 85.8 %copy-start.288 = (s32[1024]{0:T(1024)}, s32[1024]{0:T(1024)S(1)}, u32[]{:S(2)}) copy-start(s32[1024]{0:T(1024)S(1)} %pad_clamp_fusion.10) | copy-start | bytes 12292
  59.2 94.3 %copy-start.184 = (f32[128,2]{1,0:T(8,128)}, f32[128,2]{1,0:T(8,128)S(1)}, u32[]{:S(2)}) copy-start(f32[128,2]{1,0:T(8,128)S(1)} %copy.352) | copy-start | bytes 3076
  61.2 17.7 %copy-start.8 = (bf16[2,128,768]{2,1,0:T(8,128)(2,1)S(1)}, bf16[2,128,768]{2,1,0:T(8,128)(2,1)}, u32[]{:S(2)}) copy-start(bf16[2,128,768]{2,1,0:T(8,128)(2,1)} %param.19) | copy-start | bytes 1179652
  70.7 74.9 %copy-start.287 = (s32[1024]{0:T(1024)}, s32[1024]{0:T(1024)S(1)}, u32[]{:S(2)}) copy-start(s32[1024]{0:T(1024)S(1)} %pad_clamp_fusion.6) | copy-start | bytes 12292
  82.2 25.8 %copy-start.11 = (bf16[128,768]{1,0:T(8,128)(2,1)}, bf16[128,768]{1,0:T(8,128)(2,1)S(1)}, u32[]{:S(2)}) copy-start(bf16[128,768]{1,0:T(8,128)(2,1)S(1)} %get-tuple-element.233) | copy-start | bytes 589828
  82.2 25.8 %copy-start.12 = (bf16[128,768]{1,0:T(8,128)(2,1)}, bf16[128,768]{1,0:T(8,128)(2,1)S(1)}, u32[]{:S(2)}) copy-start(bf16[128,768]{1,0:T(8,128)(2,1)S(1)} %get-tuple-element.154) | copy-start | bytes 589828
  85.2 48.7 %copy-start.234 = (f32[128,2]{0,1:T(2,128)}, f32[128,2]{0,1:T(2,128)S(1)}, u32[]{:S(2)}) copy-start(f32[128,2]{0,1:T(2,128)S(1)} %select_reduce_fusion.5) | copy-start | bytes 3076
  85.3 48.7 %copy-start.273 = (f32[128]{0:T(128)}, f32[128]{0:T(128)S(1)}, u32[]{:S(2)}) copy-start(f32[128]{0:T(128)S(1)} %reduce_max.135) | copy-start | bytes 1540
  87.0 13.9 %all-to-all-start = ((bf16[8,48,768]{2,1,0:T(8,128)(2,1)}), bf16[8,48,768]{2,1,0:T(8,128)(2,1)S(1)}, u32[]{:S(2)}, u32[]{:S(2)}) async-start(bf16[8,48,768]{2,1,0:T(8,128)(2,1)} %bitcast.940), calls=%async_computation.1 | async-start | bytes 1179648 | tf_op jit(solution)/shard_map/all_to_all | solution.py:89
  91.5 42.5 %copy-start.291 = (f32[128]{0:T(128)}, f32[128]{0:T(128)S(1)}, u32[]{:S(2)}) copy-start(f32[128]{0:T(128)S(1)} %fusion.396) | copy-start | bytes 1540
  101.9 13.9 %all-to-all-start.4 = ((bf16[8,48,768]{2,1,0:T(8,128)(2,1)}), bf16[8,48,768]{2,1,0:T(8,128)(2,1)S(1)}, u32[]{:S(2)}, u32[]{:S(2)}) async-start(bf16[8,48,768]{2,1,0:T(8,128)(2,1)} %bitcast.942), calls=%async_computation.7 | async-start | bytes 1179648 | tf_op jit(solution)/shard_map/all_to_all | solution.py:89
  115.8 13.9 %all-to-all-start.1 = ((bf16[8,48,768]{2,1,0:T(8,128)(2,1)}), bf16[8,48,768]{2,1,0:T(8,128)(2,1)S(1)}, u32[]{:S(2)}, u32[]{:S(2)}) async-start(bf16[8,48,768]{2,1,0:T(8,128)(2,1)} %convolution_convert_fusion.7), calls=%async_computation.2 | async-start | bytes 1179648 | tf_op jit(solution)/shard_map/all_to_all | solution.py:98
  129.7 14.7 %all-to-all-start.5 = ((bf16[8,48,768]{2,1,0:T(8,128)(2,1)}), bf16[8,48,768]{2,1,0:T(8,128)(2,1)}, u32[]{:S(2)}, u32[]{:S(2)}) async-start(bf16[8,48,768]{2,1,0:T(8,128)(2,1)} %convolution_convert_fusion.5), calls=%async_computation.8 | async-start | bytes 1179648 | tf_op jit(solution)/shard_map/all_to_all | solution.py:98
  133.9 73.5 %reduce-scatter.11.cloned.1.call-start = ((), (), s32[]{:S(2)}) async-start(), calls=%async_computation.27 | async-start | bytes 983040 | tf_op jit(solution)/shard_map/reduce_scatter | solution.py:77
  134.1 19.4 %copy-start.135 = (f32[128,2]{1,0:T(8,128)}, f32[128,2]{1,0:T(8,128)S(1)}, u32[]{:S(2)}) copy-start(f32[128,2]{1,0:T(8,128)S(1)} %copy.347) | copy-start | bytes 3076
  183.9 49.9 %reduce-scatter.15.cloned.1.call-start = ((), (), s32[]{:S(2)}) async-start(), calls=%async_computation.29 | async-start | bytes 983040 | tf_op jit(solution)/shard_map/reduce_scatter | solution.py:77
  187.9 49.1 %copy-start.128 = (bf16[3,64,512]{2,1,0:T(8,128)(2,1)}, bf16[3,64,512]{2,1,0:T(8,128)(2,1)S(1)}, u32[]{:S(2)}) copy-start(bf16[3,64,512]{2,1,0:T(8,128)(2,1)S(1)} %fusion.108) | copy-start | bytes 589828
  189.2 47.8 %copy-start.134 = (f32[1,768,6]{1,0,2:T(1,128)S(1)}, f32[1,768,6]{1,0,2:T(1,128)}, u32[]{:S(2)}) copy-start(f32[1,768,6]{1,0,2:T(1,128)} %get-tuple-element.256) | copy-start | bytes 55300
  189.2 47.8 %copy-start.229 = (f32[128,6]{0,1:T(8,128)S(1)}, f32[128,6]{0,1:T(8,128)}, u32[]{:S(2)}) copy-start(f32[128,6]{0,1:T(8,128)} %copy-done.228) | copy-start | bytes 9220
  189.2 48.0 %copy-start.227 = (f32[128,6]{0,1:T(8,128)S(1)}, f32[128,6]{0,1:T(8,128)}, u32[]{:S(2)}) copy-start(f32[128,6]{0,1:T(8,128)} %copy-done.226) | copy-start | bytes 9220
  189.2 48.3 %copy-start.206 = (f32[2,2,768]{2,1,0:T(2,128)S(1)}, f32[2,2,768]{2,1,0:T(2,128)}, u32[]{:S(2)}) copy-start(f32[2,2,768]{2,1,0:T(2,128)} %dot_general.359) | copy-start | bytes 36868
  208.4 29.8 %copy-start.271 = (s32[128,2]{0,1:T(2,128)S(1)}, s32[128,2]{0,1:T(2,128)}, u32[]{:S(2)}) copy-start(s32[128,2]{0,1:T(2,128)} %copy-done.270) | copy-start | bytes 3076
  208.4 29.8 %copy-start.268 = (s32[128,2]{0,1:T(2,128)S(1)}, s32[128,2]{0,1:T(2,128)}, u32[]{:S(2)}) copy-start(s32[128,2]{0,1:T(2,128)} %copy-done.267) | copy-start | bytes 3076
  208.5 28.5 %copy-start.303 = (f32[128]{0:T(128)}, f32[128]{0:T(128)S(1)}, u32[]{:S(2)}) copy-start(f32[128]{0:T(128)S(1)} %add_rsqrt_fusion.4) | copy-start | bytes 1540
  208.5 30.9 %copy-start.334 = (pred[256]{0:T(512)(128)(4,1)S(1)}, pred[256]{0:T(512)(128)(4,1)}, u32[]{:S(2)}) copy-start(pred[256]{0:T(512)(128)(4,1)} %get-tuple-element.315) | copy-start | bytes 772
  237.0 25.5 %copy-start.16 = (bf16[128,768]{1,0:T(8,128)(2,1)}, bf16[128,768]{1,0:T(8,128)(2,1)S(1)}, u32[]{:S(2)}) copy-start(bf16[128,768]{1,0:T(8,128)(2,1)S(1)} %get-tuple-element.146) | copy-start | bytes 589828
  237.0 31.4 %copy-start.14 = (bf16[128,768]{1,0:T(8,128)(2,1)}, bf16[128,768]{1,0:T(8,128)(2,1)S(1)}, u32[]{:S(2)}) copy-start(bf16[128,768]{1,0:T(8,128)(2,1)S(1)} %get-tuple-element.294) | copy-start | bytes 589828
  246.2 25.6 %all-to-all-start.2 = ((bf16[8,48,768]{2,1,0:T(8,128)(2,1)}), bf16[8,48,768]{2,1,0:T(8,128)(2,1)S(1)}, u32[]{:S(2)}, u32[]{:S(2)}) async-start(bf16[8,48,768]{2,1,0:T(8,128)(2,1)} %bitcast.939), calls=%async_computation.4 | async-start | bytes 1179648 | tf_op jit(solution)/shard_map/all_to_all | solution.py:89
  272.6 14.6 %all-to-all-start.8 = ((bf16[8,48,768]{2,1,0:T(8,128)(2,1)}), bf16[8,48,768]{2,1,0:T(8,128)(2,1)S(1)}, u32[]{:S(2)}, u32[]{:S(2)}) async-start(bf16[8,48,768]{2,1,0:T(8,128)(2,1)} %bitcast.139), calls=%async_computation.12 | async-start | bytes 1179648 | tf_op jit(solution)/shard_map/all_to_all | solution.py:89
  288.2 13.9 %all-to-all-start.6 = ((bf16[8,48,768]{2,1,0:T(8,128)(2,1)}), bf16[8,48,768]{2,1,0:T(8,128)(2,1)S(1)}, u32[]{:S(2)}, u32[]{:S(2)}) async-start(bf16[8,48,768]{2,1,0:T(8,128)(2,1)} %bitcast.941), calls=%async_computation.10 | async-start | bytes 1179648 | tf_op jit(solution)/shard_map/all_to_all | solution.py:89
  303.1 13.9 %all-to-all-start.12 = ((bf16[8,48,768]{2,1,0:T(8,128)(2,1)}), bf16[8,48,768]{2,1,0:T(8,128)(2,1)S(1)}, u32[]{:S(2)}, u32[]{:S(2)}) async-start(bf16[8,48,768]{2,1,0:T(8,128)(2,1)} %bitcast.943), calls=%async_computation.18 | async-start | bytes 1179648 | tf_op jit(solution)/shard_map/all_to_all | solution.py:89
  317.0 13.9 %all-to-all-start.3 = ((bf16[8,48,768]{2,1,0:T(8,128)(2,1)}), bf16[8,48,768]{2,1,0:T(8,128)(2,1)S(1)}, u32[]{:S(2)}, u32[]{:S(2)}) async-start(bf16[8,48,768]{2,1,0:T(8,128)(2,1)} %convolution_convert_fusion.6), calls=%async_computation.5 | async-start | bytes 1179648 | tf_op jit(solution)/shard_map/all_to_all | solution.py:98
  330.9 14.2 %all-to-all-start.9 = ((bf16[8,48,768]{2,1,0:T(8,128)(2,1)}), bf16[8,48,768]{2,1,0:T(8,128)(2,1)S(1)}, u32[]{:S(2)}, u32[]{:S(2)}) async-start(bf16[8,48,768]{2,1,0:T(8,128)(2,1)} %fusion.81), calls=%async_computation.13 | async-start | bytes 1179648 | tf_op jit(solution)/shard_map/all_to_all | solution.py:98
  345.1 17.8 %all-to-all-start.7 = ((bf16[8,48,768]{2,1,0:T(8,128)(2,1)}), bf16[8,48,768]{2,1,0:T(8,128)(2,1)}, u32[]{:S(2)}, u32[]{:S(2)}) async-start(bf16[8,48,768]{2,1,0:T(8,128)(2,1)} %convolution_convert_fusion.4), calls=%async_computation.11 | async-start | bytes 1179648 | tf_op jit(solution)/shard_map/all_to_all | solution.py:98
  363.0 14.6 %all-to-all-start.13 = ((bf16[8,48,768]{2,1,0:T(8,128)(2,1)}), bf16[8,48,768]{2,1,0:T(8,128)(2,1)S(1)}, u32[]{:S(2)}, u32[]{:S(2)}) async-start(bf16[8,48,768]{2,1,0:T(8,128)(2,1)} %fusion.78), calls=%async_computation.19 | async-start | bytes 1179648 | tf_op jit(solution)/shard_map/all_to_all | solution.py:98
  367.1 70.6 %reduce-scatter.17.cloned.1.call-start = ((), (), s32[]{:S(2)}) async-start(), calls=%async_computation.30 | async-start | bytes 983040 | tf_op jit(solution)/shard_map/reduce_scatter | solution.py:77
  374.6 22.3 %copy-start.36 = (f32[128,768]{1,0:T(8,128)}, f32[128,768]{1,0:T(8,128)S(1)}, u32[]{:S(2)}) copy-start(f32[128,768]{1,0:T(8,128)S(1)} %get-tuple-element.356) | copy-start | bytes 1179652
  374.6 22.3 %copy-start.342 = (f32[128]{0:T(128)}, f32[128]{0:T(128)S(1)}, u32[]{:S(2)}) copy-start(f32[128]{0:T(128)S(1)} %broadcast_multiply_fusion.11) | copy-start | bytes 1540
  396.9 25.1 %copy-start.210 = (f32[128,6]{0,1:T(8,128)}, f32[128,6]{0,1:T(8,128)S(1)}, u32[]{:S(2)}) copy-start(f32[128,6]{0,1:T(8,128)S(1)} %select_reduce_fusion.1) | copy-start | bytes 9220
  441.8 32.4 %copy-start.25 = (f32[128,768]{1,0:T(8,128)}, f32[128,768]{1,0:T(8,128)S(1)}, u32[]{:S(2)}) copy-start(f32[128,768]{1,0:T(8,128)S(1)} %get-tuple-element.191) | copy-start | bytes 1179652
  463.7 13.9 %all-to-all-start.10 = ((bf16[8,48,768]{2,1,0:T(8,128)(2,1)}), bf16[8,48,768]{2,1,0:T(8,128)(2,1)S(1)}, u32[]{:S(2)}, u32[]{:S(2)}) async-start(bf16[8,48,768]{2,1,0:T(8,128)(2,1)} %bitcast.164), calls=%async_computation.15 | async-start | bytes 1179648 | tf_op jit(solution)/shard_map/all_to_all | solution.py:89
  467.2 35.3 %reduce-scatter.21.cloned.1.call-start = ((), (), s32[]{:S(2)}) async-start(), calls=%async_computation.32 | async-start | bytes 983040 | tf_op jit(solution)/shard_map/reduce_scatter | solution.py:77
  481.8 16.9 %all-to-all-start.11 = ((bf16[8,48,768]{2,1,0:T(8,128)(2,1)}), bf16[8,48,768]{2,1,0:T(8,128)(2,1)S(1)}, u32[]{:S(2)}, u32[]{:S(2)}) async-start(bf16[8,48,768]{2,1,0:T(8,128)(2,1)} %fusion.75), calls=%async_computation.16 | async-start | bytes 1179648 | tf_op jit(solution)/shard_map/all_to_all | solution.py:98
  516.4 26.1 %copy-start.253 = (f32[128,2,2]{0,2,1:T(2,128)}, f32[128,2,2]{0,2,1:T(2,128)S(1)}, u32[]{:S(2)}) copy-start(f32[128,2,2]{0,2,1:T(2,128)S(1)} %subtract_multiply_fusion) | copy-start | bytes 6148
  519.5 13.9 %all-to-all-start.14 = ((bf16[8,48,768]{2,1,0:T(8,128)(2,1)}), bf16[8,48,768]{2,1,0:T(8,128)(2,1)S(1)}, u32[]{:S(2)}, u32[]{:S(2)}) async-start(bf16[8,48,768]{2,1,0:T(8,128)(2,1)} %bitcast.216), calls=%async_computation.21 | async-start | bytes 1179648 | tf_op jit(solution)/shard_map/all_to_all | solution.py:89
  523.1 20.7 %copy-start.254 = (f32[128,2,2]{0,2,1:T(2,128)}, f32[128,2,2]{0,2,1:T(2,128)S(1)}, u32[]{:S(2)}) copy-start(f32[128,2,2]{0,2,1:T(2,128)S(1)} %subtract_multiply_fusion.2) | copy-start | bytes 6148
  537.9 13.9 %all-to-all-start.15 = ((bf16[8,48,768]{2,1,0:T(8,128)(2,1)}), bf16[8,48,768]{2,1,0:T(8,128)(2,1)S(1)}, u32[]{:S(2)}, u32[]{:S(2)}) async-start(bf16[8,48,768]{2,1,0:T(8,128)(2,1)} %fusion.72), calls=%async_computation.22 | async-start | bytes 1179648 | tf_op jit(solution)/shard_map/all_to_all | solution.py:98
  541.4 68.5 %reduce-scatter.23.cloned.1.call-start = ((), (), s32[]{:S(2)}) async-start(), calls=%async_computation.33 | async-start | bytes 983040 | tf_op jit(solution)/shard_map/reduce_scatter | solution.py:77
  586.5 50.1 %reduce-scatter.19.cloned.1.call-start = ((), (), s32[]{:S(2)}) async-start(), calls=%async_computation.31 | async-start | bytes 983040 | tf_op jit(solution)/shard_map/reduce_scatter | solution.py:77
  594.2 199.0 %all-reduce.23.cloned.1.call-start = ((), (), s32[]{:S(2)}) async-start(), calls=%async_computation.34 | async-start | bytes 196608 | tf_op jit(solution)/shard_map/psum | solution.py:508
  606.3 30.2 %copy-start.213 = (f32[768]{0:T(1024)S(1)}, f32[768]{0:T(1024)}, u32[]{:S(2)}) copy-start(f32[768]{0:T(1024)} %copy-done.212) | copy-start | bytes 9220
  606.3 32.8 %copy-start.252 = (f32[1,2,768]{2,0,1:T(1,128)S(1)}, f32[1,2,768]{2,0,1:T(1,128)}, u32[]{:S(2)}) copy-start(f32[1,2,768]{2,0,1:T(1,128)} %maximum_add_fusion.1) | copy-start | bytes 18436
  639.8 328.9 %all-reduce.25.cloned.1.call-start = ((), (), s32[]{:S(2)}) async-start(), calls=%async_computation.35 | async-start | bytes 9437184
  656.7 26.1 %all-to-all-start.17 = ((bf16[8,2,192,96]{3,2,1,0:T(8,128)(2,1)}), bf16[8,2,192,96]{3,2,1,0:T(8,128)(2,1)S(1)}, u32[]{:S(2)}, u32[]{:S(2)}) async-start(bf16[8,2,192,96]{3,2,1,0:T(8,128)(2,1)} %maximum_bitcast_fusion.1), calls=%async_computation.25 | async-start | bytes 1572864 | tf_op jit(solution)/shard_map/all_to_all | solution.py:24
  682.8 113.1 %all-to-all-start.16 = ((bf16[8,2,3,96,192]{3,4,2,1,0:T(8,128)(2,1)}), bf16[8,2,3,96,192]{3,4,2,1,0:T(8,128)(2,1)S(1)}, u32[]{:S(2)}, u32[]{:S(2)}) async-start(bf16[8,2,3,96,192]{3,4,2,1,0:T(8,128)(2,1)} %maximum_bitcast_fusion), calls=%async_computation.24 | async-start | bytes 4718592 | tf_op jit(solution)/shard_map/all_to_all | solution.py:24
  (324 other events, 1487.0 us)
Sparse Core Ops, SparseCore 0:
  28.1 24.1 reduce-scatter.8
  55.6 23.2 reduce-scatter.12
  184.0 23.2 reduce-scatter.10
  210.5 23.2 reduce-scatter.14
  414.3 23.2 reduce-scatter.16
  473.4 26.8 reduce-scatter.20
  586.6 23.3 reduce-scatter.22
  613.2 23.2 reduce-scatter.18
  643.2 149.9 all-reduce.22
  795.4 173.2 all-reduce.24
where the time goes:
time: 995 us; the launch traced here: 983 us
  waiting for transfers between devices  437 us (44%)
  matrix products  176 us (18%)
  local copies, waits for them, and re-layouts  118 us (12%)
  other arithmetic  92.3 us (9%)
  starting transfers between devices  70.8 us (7%)
  blocking collectives  68.5 us (7%)
  between operations  20.4 us (2%)
    unnamed x11, waiting for transfers between devices  171 us
    psum x1, waiting for transfers between devices, local(): lax.psum((stacked[0], stacked[5], stacked[6], stacked[7]), ('dp', 'expert...  99 us
    reduce_scatter x8, waiting for transfers between devices, sum_rows(): lax.psum_scatter(product(left_rows).astype(jnp.bfloat16), 'tensor', scatt...  84 us
    all_gather x8, blocking collectives, spread_rows(): return lax.all_gather(rows_low, 'tensor', axis=0, tiled=True)  68.5 us
    all_to_all x8, waiting for transfers between devices, send_rows(): lax.all_to_all(copied, ('expert', 'tensor'), split_axis=0, concat_axis=0,...  39.5 us
    all_to_all x8, waiting for transfers between devices, return_rows(): lax.all_to_all(source_slabs.astype(jnp.bfloat16), ('expert', 'tensor'), s...  34.8 us
    all_to_all x8, starting transfers between devices, return_rows(): lax.all_to_all(source_slabs.astype(jnp.bfloat16), ('expert', 'tensor'), s...  30.8 us
    all_to_all x8, starting transfers between devices, send_rows(): lax.all_to_all(copied, ('expert', 'tensor'), split_axis=0, concat_axis=0,...  29.3 us
  transfers between devices with their start and end apart: 28, of which 23 were waited for; matrix products, arithmetic and copies ran while one was open for 23% of the time, Pallas kernels for 0%

commit v1 on v0

v1 whole, which is shorter than its diff:
```python
import functools
import math

import jax
import jax.numpy as jnp
from jax import lax
from jax.experimental import pallas as pl
from jax.experimental.pallas import tpu as pltpu
from jax.sharding import PartitionSpec as P

HDIM = 64
epsilon = 1e-06
masked_value = -1e30
highest = lax.Precision.HIGHEST
low = jnp.bfloat16
full = jnp.float32
MIB = 1 << 20


def shape_of(shape, dtype):
    return jax.ShapeDtypeStruct(shape, dtype)


def run_kernel(body, outs, ins, name, limit, flops=0, scratch=()):
    in_bytes = sum(a.size * a.dtype.itemsize for a in ins)
    out_bytes = sum(math.prod(o.shape) * jnp.dtype(o.dtype).itemsize for o in outs)
    vmem = pl.BlockSpec(memory_space=pltpu.VMEM)
    return pl.pallas_call(
        body,
        out_shape=tuple(outs),
        in_specs=[vmem] * len(ins),
        out_specs=tuple([vmem] * len(outs)),
        scratch_shapes=list(scratch),
        compiler_params=pltpu.CompilerParams(vmem_limit_bytes=limit * MIB),
        cost_estimate=pl.CostEstimate(
            flops=flops, bytes_accessed=in_bytes + out_bytes, transcendentals=0
        ),
        name=name,
    )(*ins)


def dot(a, b):
    return jnp.dot(a, b, preferred_element_type=full)


def dot_nt(a, b):
    return lax.dot_general(a, b, (((1,), (1,)), ((), ())), preferred_element_type=full)


def dot_tn(a, b):
    return lax.dot_general(a, b, (((0,), (0,)), ((), ())), preferred_element_type=full)


def lanes(rows, width=128):
    return lax.broadcasted_iota(jnp.int32, (rows, width), 1)


def stack_rows(refs):
    if refs[0].shape[0] % 16:
        return jnp.concatenate([r[...].astype(full) for r in refs], axis=0).astype(low)
    return jnp.concatenate([r[...] for r in refs], axis=0)


def rms_scale(rows):
    return lax.rsqrt(jnp.mean(rows * rows, axis=-1, keepdims=True) + epsilon)


def split2(rows):
    top = rows.astype(low)
    return top, (rows - top.astype(full)).astype(low)


def norm_kernel(stream, gain, out):
    rows = stream[...].astype(full)
    out[...] = (rows * rms_scale(rows) * gain[...]).astype(low)


def half_masks():
    lane = lanes(1)
    return (lane < HDIM).astype(full).astype(low), (lane >= HDIM).astype(full).astype(low)


def swap_halves(rows):
    lane = lanes(rows.shape[0])
    half = HDIM // 2
    return jnp.where(
        lane % HDIM < half, pltpu.roll(rows, 128 - half, 1), pltpu.roll(rows, half, 1)
    )


def attn_fwd_kernel(blocks, *refs):
    heads = refs[:blocks]
    w, wo, cos, sin, bias, keep, far, send, saved, mixed, logsum = refs[blocks:]
    rows_n = keep.shape[0]
    width = 128
    h = stack_rows(heads)
    proj = dot(h, w[...])
    c = cos[...]
    s = sin[...]
    lane = lanes(proj.shape[0])

    def turn(chunk):
        return chunk * c + swap_halves(chunk) * s

    saved[:, 0:128] = (turn(proj[:, 0:128]) * 0.125).astype(low)
    saved[:, 128:256] = turn(proj[:, 128:256]).astype(low)
    saved[:, 256:384] = proj[:, 256:384].astype(low)
    third = turn(proj[:, 384:512])
    saved[:, 384:512] = jnp.where(lane < HDIM, third * 0.125, 0.0).astype(low)
    saved[:, 512:640] = jnp.where(lane < HDIM, pltpu.roll(third, HDIM, 1), 0.0).astype(low)
    saved[:, 640:768] = proj[:, 512:640].astype(low)
    first, second = half_masks()
    lane = lanes(rows_n)
    for i in range(blocks):
        part = slice(i * rows_n, (i + 1) * rows_n)
        shift = bias[part, :].astype(full)
        q01 = saved[part, 0:128]
        q2 = saved[part, 384:512]
        results = []
        sums = []
        for query, keys, values in (
            (q01 * first, slice(128, 256), slice(256, 384)),
            (q01 * second, slice(128, 256), slice(256, 384)),
            (q2, slice(512, 640), slice(640, 768)),
        ):
            scores = dot_nt(query, saved[:, keys]) + shift
            peak = jnp.max(scores, axis=-1, keepdims=True)
            exponent = jnp.exp(scores - peak)
            total = jnp.sum(exponent, axis=-1, keepdims=True)
            probs = (exponent * (1.0 / total)).astype(low)
            results.append(dot(probs, saved[:, values]))
            sums.append(peak + jnp.log(total))
        logsum[part, :] = jnp.where(lane == 0, sums[0], jnp.where(lane == 1, sums[1], sums[2]))
        mix = jnp.concatenate(
            [jnp.where(lane < HDIM, results[0], results[1]), results[2]], axis=1
        ).astype(low)
        mixed[part, :] = mix
        value = dot(mix, wo[...]).astype(low)
        if i == 0:
            keep[...] = value
        elif i == 2:
            far[...] = value
        else:
            at = (i // 2) * rows_n
            send[at : at + rows_n, :] = value


def attn_bwd_kernel(blocks, *refs):
    grads = refs[:blocks]
    (w, wo, cos, sin, bias, saved, logsum, keep, far, send, dqkv, probs_s, dscore_s, dq_s) = refs[
        blocks:
    ]
    rows_n = keep.shape[0]
    c = cos[...]
    s = sin[...]
    dattn = stack_rows(grads)
    dmix = dot_nt(dattn, wo[...]).astype(low)
    d01 = dmix[:, 0:128]
    d2 = dmix[:, 128:256]
    first, second = half_masks()
    q01 = saved[:, 0:128]
    k01 = saved[:, 128:256]
    v01 = saved[:, 256:384]
    q2 = saved[:, 384:512]
    k2 = saved[:, 512:640]
    v2 = saved[:, 640:768]
    heads = (
        (q01 * first, k01 * first, v01, d01 * first),
        (q01 * second, k01 * second, v01, d01 * second),
        (q2, k2, v2, d2),
    )
    dks = []
    dvs = []
    for n, (query, keys, values, dout) in enumerate(heads):
        for i in range(blocks):
            part = slice(i * rows_n, (i + 1) * rows_n)
            scores = dot_nt(query[part], keys) + bias[part, :].astype(full)
            probs = jnp.exp(scores - logsum[part, n : n + 1])
            dprobs = dot_nt(dout[part], values)
            inner = jnp.sum(probs * dprobs, axis=-1, keepdims=True)
            dscores = (probs * (dprobs - inner)).astype(low)
            probs_s[part, :] = probs.astype(low)
            dscore_s[part, :] = dscores
            dq = dot(dscores, keys)
            if n == 1:
                dq_s[part, 0:128] += dq
            else:
                at = 128 * (n // 2)
                dq_s[part, at : at + 128] = dq
        dks.append(dot_tn(dscore_s[...], query))
        dvs.append(dot_tn(probs_s[...], dout))

    def turn_back(chunk):
        return chunk * c - swap_halves(chunk) * s

    dqkv[:, 0:128] = turn_back(dq_s[:, 0:128] * 0.125).astype(low)
    dqkv[:, 128:256] = turn_back(dks[0] + dks[1]).astype(low)
    dqkv[:, 256:384] = (dvs[0] + dvs[1]).astype(low)
    dqkv[:, 384:512] = turn_back(
        dq_s[:, 128:256] * 0.125 + pltpu.roll(dks[2], HDIM, 1)
    ).astype(low)
    dqkv[:, 512:640] = dvs[2].astype(low)
    dh = dot_nt(dqkv[...], w[...]).astype(low)
    keep[...] = dh[0:rows_n]
    far[...] = dh[2 * rows_n : 3 * rows_n]
    send[0:rows_n, :] = dh[rows_n : 2 * rows_n]
    send[rows_n : 2 * rows_n, :] = dh[3 * rows_n : 4 * rows_n]


def attn_weights_kernel(blocks, micro, *refs):
    out = refs[-1]
    refs = refs[:-1]
    per = 2 * blocks + 2
    for m in range(micro):
        mine = refs[m * per : (m + 1) * per]
        h = stack_rows(mine[:blocks])
        d = stack_rows(mine[blocks : 2 * blocks])
        dqkv, mixed = mine[2 * blocks :]
        qkv_part = dot_tn(h, dqkv[...])
        out_part = dot_tn(d, mixed[...])
        if m:
            qkv_total = qkv_total + qkv_part
            out_total = out_total + out_part
        else:
            qkv_total, out_total = qkv_part, out_part
    out[:, 0:512] = qkv_total[:, 0:512].astype(low)
    out[:, 512:640] = (qkv_total[:, 512:640] + pltpu.roll(out_total[:, 128:256], HDIM, 1)).astype(
        low
    )
    out[:, 640:768] = out_total[:, 0:128].astype(low)


def add_far_kernel(far, arrived, out):
    rows_n = far.shape[0]
    out[...] = (far[...].astype(full) + arrived[rows_n : 2 * rows_n, :].astype(full)).astype(low)


def add_back_kernel(keep, arrived, *outs):
    total = keep[...].astype(full) + arrived[...].astype(full)
    rows_n = outs[0].shape[0]
    for i, out in enumerate(outs):
        out[...] = total[i * rows_n : (i + 1) * rows_n].astype(low)


def mid_kernel(
    experts_n,
    routes_n,
    keep,
    arrived,
    across,
    stream,
    gain,
    router,
    routes_col,
    routes_row,
    previous,
    mid,
    h_moe,
    logits_out,
    aux,
    pick,
    *bufs,
):
    rows_n = keep.shape[0]
    capacity = bufs[0].shape[0]
    rows = (
        stream[...].astype(full)
        + keep[...].astype(full)
        + arrived[0:rows_n, :].astype(full)
        + across[...].astype(full)
    )
    mid[...] = rows
    h = (rows * rms_scale(rows) * gain[...]).astype(low)
    h_moe[...] = h
    parts = dot(h, router[...])
    raw = parts[:, 0:128] + parts[:, 128:256] + parts[:, 256:384]
    lane = lanes(rows_n)
    logits = raw + previous[...]
    logits_out[...] = jnp.where(lane < routes_n, logits, 0.0)
    picked = [
        jnp.sum(jnp.where(lane == routes_col[:, k : k + 1], logits, 0.0), axis=-1, keepdims=True)
        for k in range(2)
    ]
    peak = jnp.maximum(picked[0], picked[1])
    gate = [jnp.exp(p - peak) for p in picked]
    both = gate[0] + gate[1]
    columns = [gate[0] / both, gate[1] / both]
    for j in range(2):
        pair = [raw[:, routes_n + 2 * j + i : routes_n + 2 * j + i + 1] for i in range(2)]
        peak = jnp.maximum(pair[0], pair[1])
        power = [jnp.exp(p - peak) for p in pair]
        both = power[0] + power[1]
        columns += [power[0] / both, power[1] / both]
    value = jnp.zeros((rows_n, 128), full)
    for i, column in enumerate(columns):
        value = jnp.where(lane == i, column, value)
    aux[...] = value
    index_rows = max(16, experts_n)
    expert = lax.broadcasted_iota(jnp.int32, (index_rows, rows_n), 0)
    first = routes_row[0:1, :]
    second = routes_row[1:2, :]
    member = ((first == expert) | (second == expert)).astype(full).astype(low)
    before = (
        lax.broadcasted_iota(jnp.int32, (rows_n, rows_n), 0)
        < lax.broadcasted_iota(jnp.int32, (rows_n, rows_n), 1)
    )
    rank = dot(member, before.astype(full).astype(low))
    slot = lax.broadcasted_iota(jnp.int32, (capacity, rows_n), 0).astype(full)
    picks = []
    for route in (first, second):
        picks.append(
            jnp.concatenate(
                [
                    ((slot == rank[k : k + 1, :]) & (route == k)).astype(full)
                    for k in range(experts_n)
                ],
                axis=0,
            )
        )
    pick[:, 0:rows_n] = picks[0].astype(low)
    pick[:, rows_n : 2 * rows_n] = picks[1].astype(low)
    sent = dot((picks[0] + picks[1]).astype(low), h)
    for k, buf in enumerate(bufs):
        buf[...] = sent[k * capacity : (k + 1) * capacity].astype(low)


def route_values(experts_n, pick, arrivals, aux, routes_col, h, vec):
    rows_n = h.shape[0]
    twice = jnp.concatenate([pick[...], pick[...]], axis=0)
    both = dot_tn(twice, stack_rows(arrivals))
    values = []
    for k in range(2):
        route = routes_col[:, k : k + 1]
        scale = (route == experts_n + 1).astype(full)
        value = both[k * rows_n : (k + 1) * rows_n]
        for j in range(2):
            here = (route == experts_n + 2 + j).astype(full)
            scale = scale + here * aux[:, 2 + 2 * j : 3 + 2 * j]
            value = value + (here * aux[:, 3 + 2 * j : 4 + 2 * j]) * vec[j : j + 1, :]
        values.append(value + scale * h)
    return values


def combine_kernel(experts_n, arrivals_n, last, *refs):
    arrivals = refs[:arrivals_n]
    pick, aux, routes_col, h_moe, mid, vec = refs[arrivals_n : arrivals_n + 6]
    values = route_values(
        experts_n, pick, arrivals, aux, routes_col, h_moe[...].astype(full), vec
    )
    rows = mid[...] + aux[:, 0:1] * values[0] + aux[:, 1:2] * values[1]
    if last:
        refs[-1][...] = rows.astype(low)
    else:
        gain, stream, h_next = refs[arrivals_n + 6 :]
        stream[...] = rows
        h_next[...] = (rows * rms_scale(rows) * gain[...]).astype(low)


def route_back(
    experts_n, routes_n, dstream, arrivals, pick, aux, routes_col, h_moe, vec, router_back, dnext,
    dlogits_out, dlocal, small, bufs,
):
    rows_n = dstream.shape[0]
    lane = lanes(rows_n)
    h_low = h_moe[...]
    h = h_low.astype(full)
    values = route_values(experts_n, pick, arrivals, aux, routes_col, h, vec)
    gates = [aux[:, k : k + 1] for k in range(2)]
    dgate = [jnp.sum(dstream * v, axis=-1, keepdims=True) for v in values]
    mean = gates[0] * dgate[0] + gates[1] * dgate[1]
    dlogits = dnext
    for k in range(2):
        dlogits = dlogits + jnp.where(
            lane == routes_col[:, k : k + 1], gates[k] * (dgate[k] - mean), 0.0
        )
    dlogits_out[...] = dlogits

    def gate_of(route):
        return sum(
            (routes_col[:, k : k + 1] == route).astype(full) * gates[k] for k in range(2)
        )

    along_h = jnp.sum(dstream * h, axis=-1, keepdims=True)
    scale = gate_of(experts_n + 1)
    both = dlogits
    for j in range(2):
        share = gate_of(experts_n + 2 + j)
        mix = [aux[:, 2 + 2 * j + i : 3 + 2 * j + i] for i in range(2)]
        along_v = jnp.sum(dstream * vec[j : j + 1, :], axis=-1, keepdims=True)
        dm = [share * along_h, share * along_v]
        inner = mix[0] * dm[0] + mix[1] * dm[1]
        for i in range(2):
            both = jnp.where(lane == routes_n + 2 * j + i, mix[i] * (dm[i] - inner), both)
        scale = scale + mix[0] * share
        small[24 + j : 25 + j, :] = jnp.sum((mix[1] * share) * dstream, axis=0, keepdims=True)
    dlocal[...] = scale * dstream + jnp.dot(
        both, router_back[...], precision=highest, preferred_element_type=full
    )
    top, rest = split2(both)
    small[0:24, :] = (dot_tn(top, h_low) + dot_tn(rest, h_low))[0:24]
    rows_n = h.shape[0]
    sent = dot(pick[:, 0:rows_n], (gates[0] * dstream).astype(low)) + dot(
        pick[:, rows_n : 2 * rows_n], (gates[1] * dstream).astype(low)
    )
    capacity = bufs[0].shape[0]
    for k, buf in enumerate(bufs):
        buf[...] = sent[k * capacity : (k + 1) * capacity].astype(low)


def last_back_kernel(experts_n, routes_n, arrivals_n, *refs):
    arrivals = refs[:arrivals_n]
    cotangent, pick, aux, routes_col, h_moe, vec, router_back = refs[arrivals_n : arrivals_n + 7]
    dlogits, dlocal, small, *bufs = refs[arrivals_n + 7 :]
    dstream = cotangent[...].astype(full)
    small[24:32, :] = jnp.zeros((8, small.shape[1]), full)
    route_back(
        experts_n, routes_n, dstream, arrivals, pick, aux, routes_col, h_moe, vec, router_back,
        jnp.zeros((dstream.shape[0], 128), full), dlogits, dlocal, small, bufs,
    )


def attn_norm_back(keep, arrived, across, stream, gain, dmid, dgain):
    rows_n = keep.shape[0]
    dh = (
        keep[...].astype(full)
        + arrived[0:rows_n, :].astype(full)
        + across[...].astype(full)
    )
    rows = stream[...].astype(full)
    scale = rms_scale(rows)
    unit = rows * scale
    dgain[...] = jnp.broadcast_to(jnp.sum(dh * unit, axis=0, keepdims=True), dgain.shape)
    dn = dh * gain[...]
    return dmid[...] + scale * (dn - unit * jnp.mean(dn * unit, axis=-1, keepdims=True))


def input_back_kernel(keep, arrived, across, stream, gain, dmid, dgain, out):
    out[...] = attn_norm_back(keep, arrived, across, stream, gain, dmid, dgain)


def next_back_kernel(experts_n, routes_n, arrivals_n, *refs):
    arrivals = refs[:arrivals_n]
    (keep, arrived, across, stream, gain, dmid, pick, aux, routes_col, h_moe, vec, router_back,
     dnext) = refs[arrivals_n : arrivals_n + 13]
    dgain, dstream_out, dlogits, dlocal, small, *bufs = refs[arrivals_n + 13 :]
    dstream = attn_norm_back(keep, arrived, across, stream, gain, dmid, dgain)
    dstream_out[...] = dstream
    small[24:32, :] = jnp.zeros((8, small.shape[1]), full)
    route_back(
        experts_n, routes_n, dstream, arrivals, pick, aux, routes_col, h_moe, vec, router_back,
        dnext[...], dlogits, dlocal, small, bufs,
    )


def expert_fwd_kernel(rows_in, *refs):
    blocks = refs[:rows_in]
    gate_up, down, keep, send = refs[rows_in:]
    rows = stack_rows(blocks)
    g = dot(rows, gate_up[0])
    u = dot(rows, gate_up[1])
    hidden = (g * jax.nn.sigmoid(g) * u).astype(low)
    value = dot(hidden, down[...]).astype(low)
    half = keep.shape[0]
    keep[...] = value[0:half]
    send[...] = value[half:]


def expert_bwd_kernel(rows_in, *refs):
    rows = stack_rows(refs[:rows_in])
    grads = stack_rows(refs[rows_in : 2 * rows_in])
    gate_up, down, keep, send, hidden_out, dgu_out = refs[2 * rows_in :]
    g = dot(rows, gate_up[0])
    u = dot(rows, gate_up[1])
    dhidden = dot_nt(grads, down[...])
    s = jax.nn.sigmoid(g)
    silu = g * s
    hidden_out[...] = (silu * u).astype(low)
    dg = (dhidden * u * s * (1.0 + g * (1.0 - s))).astype(low)
    du = (dhidden * silu).astype(low)
    width = g.shape[1]
    dgu_out[:, 0:width] = dg
    dgu_out[:, width : 2 * width] = du
    value = (dot_nt(dg, gate_up[0]) + dot_nt(du, gate_up[1])).astype(low)
    half = keep.shape[0]
    keep[...] = value[0:half]
    send[...] = value[half:]


def expert_weights_kernel(rows_in, micro, *refs):
    out = refs[-1]
    per = 2 * rows_in + 2
    groups = [refs[m * per : (m + 1) * per] for m in range(micro)]
    rows = jnp.concatenate([stack_rows(g[:rows_in]) for g in groups], axis=0)
    grads = jnp.concatenate([stack_rows(g[rows_in : 2 * rows_in]) for g in groups], axis=0)
    hidden = jnp.concatenate([g[2 * rows_in][...] for g in groups], axis=0)
    dgu = jnp.concatenate([g[2 * rows_in + 1][...] for g in groups], axis=0)
    width = dgu.shape[1]
    out[:, 0:width] = dot_tn(rows, dgu).astype(low)
    out[:, width : width + hidden.shape[1]] = dot_tn(grads, hidden).astype(low)


def expert_norm_back_kernel(arrivals_n, *refs):
    arrivals = refs[:arrivals_n]
    pick, dlocal, mid, gain, dstream, dmid, dattn, dgain = refs[arrivals_n:]
    rows_n = mid.shape[0]
    both = pick[:, 0:rows_n] + pick[:, rows_n : 2 * rows_n]
    twice = jnp.concatenate([both, both], axis=0)
    dh = dlocal[...] + dot_tn(twice, stack_rows(arrivals))
    rows = mid[...]
    scale = rms_scale(rows)
    unit = rows * scale
    dgain[...] = jnp.broadcast_to(jnp.sum(dh * unit, axis=0, keepdims=True), dgain.shape)
    dn = dh * gain[...]
    value = dstream[...].astype(full) + scale * (
        dn - unit * jnp.mean(dn * unit, axis=-1, keepdims=True)
    )
    dmid[...] = value
    dattn[...] = value.astype(low)


def swap(x, axis, k):
    n = lax.axis_size(axis)
    return lax.ppermute(x, axis, [(i, i ^ k) for i in range(n)])


def swap_pair(x, k, j):
    experts_n = lax.axis_size("expert")
    tensor_n = lax.axis_size("tensor")
    if j == 0:
        return swap(x, "expert", k)
    if k == 0:
        return swap(x, "tensor", j)
    table = [
        (e * tensor_n + t, (e ^ k) * tensor_n + (t ^ j))
        for e in range(experts_n)
        for t in range(tensor_n)
    ]
    return lax.ppermute(x, ("expert", "tensor"), table)


def gather_pack(block):
    near = swap(block, "tensor", 1)
    far = swap(block, "tensor", 2)
    return [block, near, far, swap(far, "tensor", 1)]


def sum_pack(keep, far, send):
    arrived = swap(send, "tensor", 1)
    (total,) = run_kernel(
        add_far_kernel, [shape_of(far.shape, low)], [far, arrived], "add_far", 8
    )
    return keep, arrived, swap(total, "tensor", 2)


def send_rows(bufs):
    experts_n = len(bufs)
    held = []
    for j in (0, 2):
        for k in range(experts_n):
            held.append(bufs[k] if (j, k) == (0, 0) else swap_pair(bufs[k], k, j))
    return held + [swap(x, "tensor", 1) for x in held]


def return_rows(keep, send, capacity):
    experts_n = lax.axis_size("expert")
    arrived = swap(send, "tensor", 1)
    sums = run_kernel(
        add_back_kernel,
        [shape_of((capacity, keep.shape[1]), low)] * (2 * experts_n),
        [keep, arrived],
        "add_back",
        8,
    )
    out = []
    for j in (0, 2):
        for k in range(experts_n):
            part = sums[(j // 2) * experts_n + k]
            out.append(part if (j, k) == (0, 0) else swap_pair(part, k, j))
    return out


def sum_all(rows):
    for axis in ("tensor", "expert", "dp"):
        bit = 1
        while bit < lax.axis_size(axis):
            rows = rows + swap(rows, axis, bit)
            bit *= 2
    return rows


def sum_owner(grad, axis):
    n = lax.axis_size(axis)
    here = lax.axis_index(axis)

    def piece(k):
        return lax.dynamic_index_in_dim(grad, here ^ k, 0, keepdims=False)

    pieces = [piece(0)] + [swap(piece(k), axis, k) for k in range(1, n)]
    return functools.reduce(lambda a, b: a + b, [p.astype(full) for p in pieces])


def pack_tables(row_order, lengths, width):
    tensor_n = lax.axis_size("tensor")
    mine = lax.axis_index("tensor")
    micro_n, seq = row_order.shape
    cut = row_order.reshape(micro_n, tensor_n, seq // tensor_n)
    order = jnp.concatenate(
        [
            lax.dynamic_index_in_dim(cut, mine ^ j, 1, keepdims=False)
            for j in range(tensor_n)
        ],
        axis=1,
    )
    starts = jnp.cumsum(lengths, axis=1, dtype=jnp.int32) - lengths
    reached = order[:, :, None] >= starts[:, None, :]
    begin = jnp.max(jnp.where(reached, starts[:, None, :], 0), axis=2)
    half = HDIM // 2
    lane = jnp.arange(width, dtype=jnp.int32)
    frequency = jnp.exp(
        -math.log(10000.0) * (lane % half).astype(full) / half
    )
    angles = (order - begin).astype(full)[:, :, None] * frequency[None, None, :]
    sign = jnp.where(lane % HDIM < half, -1.0, 1.0)
    allowed = (begin[:, :, None] <= order[:, None, :]) & (order[:, None, :] <= order[:, :, None])
    bias = jnp.where(allowed, 0.0, masked_value).astype(low)
    return jnp.cos(angles), jnp.sin(angles) * sign, bias


def local(
    tokens,
    cotangent,
    row_order,
    lengths,
    routes,
    norm_gains,
    w_qkv,
    w_out,
    w_gate_up,
    w_down,
    w_router,
    const_proj,
    const_vec,
):
    layers = w_qkv.shape[0]
    micro_n, rows_n, model = tokens.shape
    routes_n = w_router.shape[2]
    experts_n = lax.axis_size("expert")
    tensor_n = lax.axis_size("tensor")
    dp_n = lax.axis_size("dp")
    capacity = 9 * rows_n // (4 * (experts_n + 4))
    heads_width = w_qkv.shape[3]
    hidden_n = w_down.shape[2]
    seq = tensor_n * rows_n
    expert_rows = 2 * experts_n * capacity
    assert tensor_n == 4 and heads_width == 3 * HDIM and rows_n == 128

    cos, sin, bias = pack_tables(row_order[:, 0], lengths[:, 0], 128)
    pair = 2 * HDIM
    w_cat = jnp.concatenate(
        [
            w_qkv[:, 0, :, :pair],
            w_qkv[:, 1, :, :pair],
            w_qkv[:, 2, :, :pair],
            w_qkv[:, 0, :, pair:],
            w_qkv[:, 1, :, pair:],
            w_qkv[:, 2, :, pair:],
            jnp.zeros((layers, model, HDIM), low),
        ],
        axis=-1,
    )
    w_mix = jnp.pad(w_out, ((0, 0), (0, HDIM), (0, 0)))
    router = jnp.concatenate([w_router, const_proj], axis=-1)
    router = jnp.pad(router, ((0, 0), (0, 0), (0, 128 - router.shape[-1])))
    top = lax.reduce_precision(router, 8, 7)
    middle = lax.reduce_precision(router - top, 8, 7)
    router_low = jnp.concatenate([top, middle, router - top - middle], axis=-1).astype(low)
    router_back = jnp.swapaxes(router, 1, 2)
    relative = jnp.where(routes < experts_n, routes ^ lax.axis_index("expert"), routes)
    routes_row = jnp.swapaxes(relative, 2, 3)
    gains = norm_gains.reshape(layers, 2, 1, model)

    def fwd_layer(m, l, stream, h, previous):
        hs = gather_pack(h)
        keep, far, send, saved, mixed, logsum = run_kernel(
            functools.partial(attn_fwd_kernel, tensor_n),
            [
                shape_of((rows_n, model), low),
                shape_of((rows_n, model), low),
                shape_of((2 * rows_n, model), low),
                shape_of((seq, 768), low),
                shape_of((seq, 256), low),
                shape_of((seq, 128), full),
            ],
            [*hs, w_cat[l], w_mix[l], cos[m], sin[m], bias[m]],
            "attn_fwd",
            24,
            flops=2 * seq * model * 1024 + 12 * seq * seq * 128,
        )
        mid, h_moe, logits, aux, pick, *bufs = run_kernel(
            functools.partial(mid_kernel, experts_n, routes_n),
            [
                shape_of((rows_n, model), full),
                shape_of((rows_n, model), low),
                shape_of((rows_n, 128), full),
                shape_of((rows_n, 128), full),
                shape_of((experts_n * capacity, 2 * rows_n), low),
            ]
            + [shape_of((capacity, model), low)] * experts_n,
            [
                *sum_pack(keep, far, send),
                stream,
                gains[l, 1],
                router_low[l],
                routes[l, m],
                routes_row[l, m],
                previous,
            ],
            "mid",
            16,
            flops=4 * rows_n * model * 384,
        )
        held = send_rows(bufs)
        keep, send = run_kernel(
            functools.partial(expert_fwd_kernel, len(held)),
            [shape_of((expert_rows, model), low)] * 2,
            [*held, w_gate_up[l, 0], w_down[l, 0]],
            "expert_fwd",
            24,
            flops=2 * 2 * expert_rows * model * 3 * hidden_n,
        )
        arrivals = return_rows(keep, send, capacity)
        last = l == layers - 1
        common = [
            *arrivals, pick, aux, routes[l, m], h_moe, mid, const_vec[l],
        ]
        if last:
            (out,) = run_kernel(
                functools.partial(combine_kernel, experts_n, len(arrivals), True),
                [shape_of((rows_n, model), low)],
                common,
                "combine_last",
                16,
                flops=4 * rows_n * model * 256,
            )
            h_next = None
        else:
            out, h_next = run_kernel(
                functools.partial(combine_kernel, experts_n, len(arrivals), False),
                [shape_of((rows_n, model), full), shape_of((rows_n, model), low)],
                [*common, gains[l + 1, 0]],
                "combine",
                16,
                flops=4 * rows_n * model * 256,
            )
        kept = dict(
            hs=hs, saved=saved, mixed=mixed, logsum=logsum, mid=mid, h_moe=h_moe, aux=aux,
            pick=pick, held=held, arrivals=arrivals, stream=stream,
        )
        return out, h_next, logits, kept

    def route_outs():
        return [
            shape_of((rows_n, 128), full),
            shape_of((rows_n, model), full),
            shape_of((32, model), full),
        ] + [shape_of((capacity, model), low)] * experts_n

    def bwd_moe(m, l, kept, dstream, dlocal, bufs):
        grads = send_rows(bufs)
        keep, send, hidden, dgu = run_kernel(
            functools.partial(expert_bwd_kernel, len(grads)),
            [shape_of((expert_rows, model), low)] * 2
            + [
                shape_of((2 * expert_rows, hidden_n), low),
                shape_of((2 * expert_rows, 2 * hidden_n), low),
            ],
            [*kept["held"], *grads, w_gate_up[l, 0], w_down[l, 0]],
            "expert_bwd",
            32,
            flops=2 * 2 * expert_rows * model * 5 * hidden_n,
        )
        arrivals = return_rows(keep, send, capacity)
        dmid, dattn, dgain = run_kernel(
            functools.partial(expert_norm_back_kernel, len(arrivals)),
            [
                shape_of((rows_n, model), full),
                shape_of((rows_n, model), low),
                shape_of((8, model), full),
            ],
            [*arrivals, kept["pick"], dlocal, kept["mid"], gains[l, 1], dstream],
            "expert_norm_back",
            16,
            flops=4 * rows_n * model * 128,
        )
        return dmid, dattn, dgain, [*kept["held"], *grads, hidden, dgu]

    def bwd_attn(m, l, kept, dattn):
        ds = gather_pack(dattn)
        keep, far, send, dqkv = run_kernel(
            functools.partial(attn_bwd_kernel, tensor_n),
            [
                shape_of((rows_n, model), low),
                shape_of((rows_n, model), low),
                shape_of((2 * rows_n, model), low),
                shape_of((seq, 640), low),
            ],
            [
                *ds, w_cat[l], w_mix[l], cos[m], sin[m], bias[m], kept["saved"], kept["logsum"],
            ],
            "attn_bwd",
            32,
            flops=2 * seq * model * 1024 + 30 * seq * seq * 128,
            scratch=[
                pltpu.VMEM((seq, seq), low),
                pltpu.VMEM((seq, seq), low),
                pltpu.VMEM((seq, 256), full),
            ],
        )
        parts = sum_pack(keep, far, send)
        return parts, [*kept["hs"], *ds, dqkv, kept["mixed"]]

    micro = range(micro_n)
    streams = [tokens[m] for m in micro]
    hs = [
        run_kernel(
            norm_kernel, [shape_of((rows_n, model), low)], [tokens[m], gains[0, 0]], "norm", 8
        )[0]
        for m in micro
    ]
    zero_logits = jnp.zeros((rows_n, 128), full)
    logits = [zero_logits for _ in micro]
    kept = [[None] * layers for _ in micro]
    for l in range(layers):
        for m in micro:
            streams[m], hs[m], logits[m], kept[m][l] = fwd_layer(
                m, l, streams[m], hs[m], logits[m]
            )
    outputs = jnp.stack(streams)

    dstream = [cotangent[m] for m in micro]
    dlogits = [None] * micro_n
    smalls = []
    attn_grads = [None] * layers
    expert_grads = [None] * layers
    parts = [None] * micro_n
    dmids = [None] * micro_n
    attn_gain = [None] * layers
    for l in reversed(range(layers)):
        weights_in = []
        small_here = []
        for m in micro:
            k = kept[m][l]
            tail = [k["pick"], k["aux"], routes[l, m], k["h_moe"], const_vec[l], router_back[l]]
            if l == layers - 1:
                dlogits[m], dlocal, small, *bufs = run_kernel(
                    functools.partial(
                        last_back_kernel, experts_n, routes_n, len(k["arrivals"])
                    ),
                    route_outs(),
                    [*k["arrivals"], cotangent[m], *tail],
                    "last_back",
                    24,
                    flops=8 * rows_n * model * 256,
                )
            else:
                dgain, dstream[m], dlogits[m], dlocal, small, *bufs = run_kernel(
                    functools.partial(
                        next_back_kernel, experts_n, routes_n, len(k["arrivals"])
                    ),
                    [shape_of((8, model), full), shape_of((rows_n, model), full)]
                    + route_outs(),
                    [
                        *k["arrivals"],
                        *parts[m],
                        kept[m][l + 1]["stream"],
                        gains[l + 1, 0],
                        dmids[m],
                        *tail,
                        dlogits[m],
                    ],
                    "next_back",
                    24,
                    flops=8 * rows_n * model * 256,
                )
                attn_gain[l + 1] = dgain if m == 0 else attn_gain[l + 1] + dgain
            dmids[m], dattn, dgain, for_weights = bwd_moe(m, l, k, dstream[m], dlocal, bufs)
            weights_in.append((for_weights, dattn))
            small_here.append((small, dgain))
        (expert_grads[l],) = run_kernel(
            functools.partial(expert_weights_kernel, len(kept[0][l]["held"]), micro_n),
            [shape_of((model, 3 * hidden_n), low)],
            [x for for_weights, _ in weights_in for x in for_weights],
            "expert_weights",
            32,
            flops=2 * 2 * expert_rows * micro_n * model * 3 * hidden_n,
        )
        smalls.append(
            (
                sum(s for s, _ in small_here),
                sum(g for _, g in small_here),
            )
        )
        attn_in = []
        for m in micro:
            parts[m], more = bwd_attn(m, l, kept[m][l], weights_in[m][1])
            attn_in += more
        (attn_grads[l],) = run_kernel(
            functools.partial(attn_weights_kernel, tensor_n, micro_n),
            [shape_of((model, 768), low)],
            attn_in,
            "attn_weights",
            32,
            flops=2 * seq * micro_n * model * 768,
        )
    smalls = smalls[::-1]
    grad_inputs = []
    for m in micro:
        dgain, out = run_kernel(
            input_back_kernel,
            [shape_of((8, model), full), shape_of((rows_n, model), full)],
            [*parts[m], tokens[m], gains[0, 0], dmids[m]],
            "input_back",
            16,
        )
        attn_gain[0] = dgain if m == 0 else attn_gain[0] + dgain
        grad_inputs.append(out)

    small = [
        sum_all(jnp.concatenate([s[: routes_n + 4], s[24:26], g[0:1]], axis=0))
        for s, g in smalls
    ]
    gain_sums = [sum_all(g[0:1]) for g in attn_gain]
    grad_qkv = []
    grad_out = []
    grad_gate_up = []
    grad_down = []
    for l in range(layers):
        g = expert_grads[l].reshape(dp_n, model // dp_n, 3 * hidden_n)
        total = sum_owner(g, "dp")
        grad_gate_up.append(
            jnp.stack([total[:, :hidden_n], total[:, hidden_n : 2 * hidden_n]])[None]
        )
        grad_down.append(total[:, 2 * hidden_n :].T[None])
        g = attn_grads[l].reshape(dp_n, experts_n, model // (dp_n * experts_n), 768)
        g = sum_owner(jnp.swapaxes(g, 0, 1), "expert").astype(low)
        total = sum_owner(g, "dp")
        grad_qkv.append(
            jnp.stack(
                [
                    jnp.concatenate([total[:, 0:128], total[:, 384:448]], axis=1),
                    jnp.concatenate([total[:, 128:256], total[:, 448:512]], axis=1),
                    jnp.concatenate([total[:, 256:384], total[:, 512:576]], axis=1),
                ]
            )
        )
        grad_out.append(jnp.concatenate([total[:, 640:768], total[:, 576:640]], axis=1).T)
    small = jnp.stack(small)
    return (
        outputs,
        jnp.stack(grad_inputs),
        jnp.concatenate(gain_sums, axis=0),
        small[:, routes_n + 6],
        jnp.stack(grad_qkv),
        jnp.stack(grad_out),
        jnp.stack(grad_gate_up),
        jnp.stack(grad_down),
        jnp.swapaxes(small[:, :routes_n], 1, 2),
        jnp.swapaxes(small[:, routes_n : routes_n + 4], 1, 2),
        small[:, routes_n + 4 : routes_n + 6],
    )


def solution(mesh):
    return jax.shard_map(
        local,
        mesh=mesh,
        in_specs=(
            P(None, ("dp", "expert", "tensor"), None),
            P(None, ("dp", "expert", "tensor"), None),
            P(None, ("dp", "expert"), None),
            P(None, ("dp", "expert"), None),
            P(None, None, ("dp", "expert", "tensor"), None),
            P(),
            P(None, None, None, "tensor"),
            P(None, "tensor", None),
            P(None, "expert", None, None, "tensor"),
            P(None, "expert", "tensor", None),
            P(),
            P(),
            P(),
        ),
        out_specs=(
            P(None, ("dp", "expert", "tensor"), None),
            P(None, ("dp", "expert", "tensor"), None),
            P(),
            P(),
            P(None, None, ("dp", "expert"), "tensor"),
            P(None, "tensor", ("dp", "expert")),
            P(None, "expert", None, "dp", "tensor"),
            P(None, "expert", "tensor", "dp"),
            P(),
            P(),
            P(),
        ),
        check_vma=False,
    )
```

time: 995 us -> 511 us (0.51)
  waiting for transfers between devices: 437 us -> 149 us
  matrix products: 176 us -> 0 us
  Pallas kernels: 0 us -> 107 us
  other arithmetic: 92.3 us -> 14.4 us
  blocking collectives: 68.5 us -> 0 us
  starting transfers between devices: 70.8 us -> 128 us
  local copies, waits for them, and re-layouts: 118 us -> 102 us
  between operations: 20.4 us -> 4.65 us
    dot_general x100 -> x0, matrix products: 173 us -> none  [the longest x4 26 us: layer_forward(): jnp.einsum('qkj,qjd->qkd', const_pick, const_out, precision=highest)]
    unnamed x11 -> x0, waiting for transfers between devices: 171 us -> none
    ppermute x0 -> x162, waiting for transfers between devices: none -> 149 us  [the longest x146 134 us: swap(): return lax.ppermute(x, axis, [(i, i ^ k) for i in range(n)])]
    ppermute x0 -> x162, starting transfers between devices: none -> 128 us  [the longest x146 103 us: swap(): return lax.ppermute(x, axis, [(i, i ^ k) for i in range(n)])]
    pallas_call x0 -> x56, Pallas kernels: none -> 107 us  [run_kernel(): pl.pallas_call(body, out_shape=tuple(outs), in_specs=[vmem] * len(ins), o...]
    psum x1 -> x0, waiting for transfers between devices: 99 us -> none  [local(): lax.psum((stacked[0], stacked[5], stacked[6], stacked[7]), ('dp', 'expert...]
    reduce_scatter x8 -> x0, waiting for transfers between devices: 84 us -> none  [sum_rows(): lax.psum_scatter(product(left_rows).astype(jnp.bfloat16), 'tensor', scatt...]
    all_to_all x18 -> x0, waiting for transfers between devices: 82.3 us -> none  [the longest x8 39.5 us: send_rows(): lax.all_to_all(copied, ('expert', 'tensor'), split_axis=0, concat_axis=0,...]
  transfers between devices with their start and end apart: 28 -> 162, of which waited for: 23 -> 55; matrix products, arithmetic and copies ran while one was open for 23% -> 10% of each run, Pallas kernels for 0% -> 21%
where the time goes in v1:
time: 511 us; the launch traced here: 505 us
  waiting for transfers between devices  149 us (29%)
  starting transfers between devices  128 us (25%)
  Pallas kernels  107 us (21%)
  local copies, waits for them, and re-layouts  102 us (20%)
  other arithmetic  14.4 us (3%)
    ppermute x146, waiting for transfers between devices, swap(): return lax.ppermute(x, axis, [(i, i ^ k) for i in range(n)])  134 us
    pallas_call x56, Pallas kernels, run_kernel(): pl.pallas_call(body, out_shape=tuple(outs), in_specs=[vmem] * len(ins), o...  107 us
    ppermute x146, starting transfers between devices, swap(): return lax.ppermute(x, axis, [(i, i ^ k) for i in range(n)])  103 us
    unnamed x676, local copies, waits for them, and re-layouts  75.3 us
    ppermute x16, starting transfers between devices, swap_pair(): return lax.ppermute(x, ('expert', 'tensor'), table)  24.7 us
    ppermute x16, waiting for transfers between devices, swap_pair(): return lax.ppermute(x, ('expert', 'tensor'), table)  14.7 us
  transfers between devices with their start and end apart: 162, of which 55 were waited for; matrix products, arithmetic and copies ran while one was open for 10% of the time, Pallas kernels for 21%

profile of v1, /device:TPU:0, one launch (start us, length us, event | category | flops | bytes accessed | tf_op | source)
XLA Modules:
  0.0 505.5 jit_solution(15273798473302082859)
XLA Ops:
  3.2 3.0 collective-permute-start.33
  10.1 2.2 fusion.25
  15.1 1.8 fusion.10
  18.4 2.2 copy.91
  20.6 1.9 copy.90
  23.5 5.4 %concatenate.58 = bf16[2,768,640]{2,1,0:T(8,128)(2,1)} concatenate(bf16[2,768,128]{2,1,0:T(8,128)(2,1)} %bitcast.235, bf16[2,768,128]{2,1,0:T(8,128)(2,1)} %bitcast.234, bf16[2,768,128]{2,1,0:T(8,128)(2,1)} %bitcast.233, bf16[2,768,64]{2,1,0:T(8,128)(2,1)} %bitcast.232, bf16[2,768,64]{2,1,0:T(8,128)(2,1)} %bitcast.231, bf16[2,768,64]{2,1,0:T(8,128)(2,1)} %bitcast.230, ...), dimensions={2} | concatenate | bytes 3932160 | tf_op jit(solution)/shard_map/concatenate | solution.py:659
  28.9 2.6 slice_bitcast_fusion.2
  33.9 1.9 fusion.8
  37.4 5.9 %attn_fwd.4 = (bf16[128,768]{1,0:T(8,128)(2,1)S(1)}, bf16[128,768]{1,0:T(8,128)(2,1)S(1)}, bf16[256,768]{1,0:T(8,128)(2,1)S(1)}, bf16[512,768]{1,0:T(8,128)(2,1)...) custom-call(bf16[128,768]{1,0:T(8,128)(2,1)S(1)} %norm.2.refs_0_, ...), custom_call_target="tpu_custom_call" | custom-call | flops 1207959552 | bytes 5308416 | tf_op jit(solution)/shard_map/attn_fwd/pallas_call | solution.py:28
  46.8 6.6 %attn_fwd.6 = (bf16[128,768]{1,0:T(8,128)(2,1)S(1)}, bf16[128,768]{1,0:T(8,128)(2,1)S(1)}, bf16[256,768]{1,0:T(8,128)(2,1)}, bf16[512,768]{1,0:T(8,128)(2,1)S(1)...) custom-call(bf16[128,768]{1,0:T(8,128)(2,1)S(1)} %norm.3.refs_0_.refs_10_, ...), custom_call_target="tpu_custom_call" | custom-call | flops 1207959552 | bytes 5308416 | tf_op jit(solution)/shard_map/attn_fwd/pallas_call | solution.py:28
  55.3 1.9 collective-permute-start.4
  58.2 4.4 collective-permute-done.4.across
  65.6 2.6 collective-permute-start.7
  69.1 3.4 slice_bitcast_fusion
  77.3 1.9 expert_fwd.4
  82.1 2.0 mid.6
  88.4 2.0 collective-permute-done.39.refs_3_.refs_21_
  110.3 3.4 collective-permute-done.46.refs_2_
  118.1 3.5 collective-permute-done.49.refs_2_.refs_12_
  121.7 5.9 %attn_fwd.5 = (bf16[128,768]{1,0:T(8,128)(2,1)S(1)}, bf16[128,768]{1,0:T(8,128)(2,1)S(1)}, bf16[256,768]{1,0:T(8,128)(2,1)S(1)}, bf16[512,768]{1,0:T(8,128)(2,1)...) custom-call(bf16[128,768]{1,0:T(8,128)(2,1)S(1)} %get-tuple-element.190.refs_0_, ...), custom_call_target="tpu_custom_call" | custom-call | flops 1207959552 | bytes 5308416 | tf_op jit(solution)/shard_map/attn_fwd/pallas_call | solution.py:28
  130.5 6.8 %attn_fwd.7 = (bf16[128,768]{1,0:T(8,128)(2,1)S(1)}, bf16[128,768]{1,0:T(8,128)(2,1)S(1)}, bf16[256,768]{1,0:T(8,128)(2,1)}, bf16[512,768]{1,0:T(8,128)(2,1)S(1)...) custom-call(bf16[128,768]{1,0:T(8,128)(2,1)S(1)} %get-tuple-element.223.refs_0_.refs_10_, ...), custom_call_target="tpu_custom_call" | custom-call | flops 1207959552 | bytes 5308416 | tf_op jit(solution)/shard_map/attn_fwd/pallas_call | solution.py:28
  142.9 4.5 collective-permute-done.20.across
  151.6 2.6 mid.5
  164.7 1.9 expert_fwd.5
  175.7 2.6 mid.7
  181.8 2.0 collective-permute-done.55.refs_3_.refs_21_
  198.8 2.3 last_back.2
  205.4 2.7 last_back.3
  216.8 2.1 expert_bwd.4
  220.9 2.1 expert_bwd.6
  274.6 2.1 expert_weights.3
  276.7 2.7 collective-permute-start.147
  281.6 7.6 %attn_bwd.4 = (bf16[128,768]{1,0:T(8,128)(2,1)S(1)}, bf16[128,768]{1,0:T(8,128)(2,1)S(1)}, bf16[256,768]{1,0:T(8,128)(2,1)S(1)}, bf16[512,640]{1,0:T(8,128)(2,1)S(1)}) custom-call(bf16[128,768]{1,0:T(8,128)(2,1)} %get-tuple-element.250.refs_0_.refs_4_, bf16[128,768]{1,0:T(8,128)(2,1)S(1)} %collective-permute-done.75.refs_1_.refs_5_, ...), custom_call_target="tpu_custom_call" | custom-call | flops 1811939328 | bytes 5701632 | tf_op jit(solution)/shard_map/attn_bwd/pallas_call | solution.py:28
  289.6 7.3 %attn_bwd.6 = (bf16[128,768]{1,0:T(8,128)(2,1)S(1)}, bf16[128,768]{1,0:T(8,128)(2,1)S(1)}, bf16[256,768]{1,0:T(8,128)(2,1)S(1)}, bf16[512,640]{1,0:T(8,128)(2,1)S(1)}) custom-call(bf16[128,768]{1,0:T(8,128)(2,1)} %get-tuple-element.285.refs_0_.refs_14_, bf16[128,768]{1,0:T(8,128)(2,1)S(1)} %collective-permute-done.107.refs_1_.refs_15_, ...), custom_call_target="tpu_custom_call" | custom-call | flops 1811939328 | bytes 5701632 | tf_op jit(solution)/shard_map/attn_bwd/pallas_call | solution.py:28
  303.4 3.2 attn_weights.3
  306.8 2.3 collective-permute-done.79.refs_6_
  310.6 2.7 next_back.2
  313.5 2.7 next_back.3
  316.1 8.9 %collective-permute-done.159 = bf16[192,1536]{1,0:T(8,128)(2,1)S(1)} collective-permute-done((bf16[192,1536]{1,0:T(8,128)(2,1)S(1)}, bf16[192,1536]{1,0:T(8,128)(2,1)S(1)}, u32[]{:S(2)}, u32[]{:S(2)}) %collective-permute-start.159) | collective-permute-done | bytes 589856 | tf_op jit(solution)/shard_map/ppermute | solution.py:523
  326.2 25.9 %collective-permute-done.160 = bf16[192,1536]{1,0:T(8,128)(2,1)S(1)} collective-permute-done((bf16[192,1536]{1,0:T(8,128)(2,1)S(1)}, bf16[192,1536]{1,0:T(8,128)(2,1)S(1)}, u32[]{:S(2)}, u32[]{:S(2)}) %collective-permute-start.160) | collective-permute-done | bytes 589856 | tf_op jit(solution)/shard_map/ppermute | solution.py:523
  354.0 2.0 collective-permute-done.134
  358.8 2.2 collective-permute-start.154
  362.2 3.0 collective-permute-done.136
  365.2 3.0 collective-permute-start.137
  378.1 1.8 collective-permute-done.114.refs_11_.refs_29_
  382.1 2.1 expert_bwd.5
  384.4 2.1 expert_bwd.7
  400.7 3.4 collective-permute-done.139
  404.8 3.4 collective-permute-done.140
  408.9 2.0 expert_weights.2
  415.2 2.4 collective-permute-start.158
  419.2 4.8 collective-permute-done.92.refs_2_.refs_6_
  424.9 4.8 collective-permute-done.124.refs_2_.refs_16_
  431.6 6.3 %attn_bwd.5 = (bf16[128,768]{1,0:T(8,128)(2,1)S(1)}, bf16[128,768]{1,0:T(8,128)(2,1)S(1)}, bf16[256,768]{1,0:T(8,128)(2,1)S(1)}, bf16[512,640]{1,0:T(8,128)(2,1)S(1)}) custom-call(bf16[128,768]{1,0:T(8,128)(2,1)S(1)} %get-tuple-element.268.refs_0_.refs_4_, bf16[128,768]{1,0:T(8,128)(2,1)S(1)} %collective-permute-done.91.refs_1_.refs_5_, ...), custom_call_target="tpu_custom_call" | custom-call | flops 1811939328 | bytes 5701632 | tf_op jit(solution)/shard_map/attn_bwd/pallas_call | solution.py:28
  438.0 6.3 %attn_bwd.7 = (bf16[128,768]{1,0:T(8,128)(2,1)S(1)}, bf16[128,768]{1,0:T(8,128)(2,1)S(1)}, bf16[256,768]{1,0:T(8,128)(2,1)S(1)}, bf16[512,640]{1,0:T(8,128)(2,1)S(1)}) custom-call(bf16[128,768]{1,0:T(8,128)(2,1)S(1)} %get-tuple-element.303.refs_0_.refs_14_, bf16[128,768]{1,0:T(8,128)(2,1)S(1)} %collective-permute-done.123.refs_1_.refs_15_, ...), custom_call_target="tpu_custom_call" | custom-call | flops 1811939328 | bytes 5701632 | tf_op jit(solution)/shard_map/attn_bwd/pallas_call | solution.py:28
  444.9 21.0 %collective-permute-done.157 = bf16[192,1536]{1,0:T(8,128)(2,1)S(1)} collective-permute-done((bf16[192,1536]{1,0:T(8,128)(2,1)S(1)}, bf16[192,1536]{1,0:T(8,128)(2,1)S(1)}, u32[]{:S(2)}, u32[]{:S(2)}) %collective-permute-start.157) | collective-permute-done | bytes 589856 | tf_op jit(solution)/shard_map/ppermute | solution.py:523
  467.8 2.1 attn_weights.2
  473.0 2.7 collective-permute-done.95.across
  481.0 2.0 collective-permute-done.129
  483.9 2.8 collective-permute-done.130
  486.7 2.1 collective-permute-start.149
  488.8 2.3 collective-permute-start.151
  491.1 3.0 collective-permute-start.132
  495.0 7.6 %collective-permute-done.132 = f32[1,768]{1,0:T(1,128)S(1)} collective-permute-done((f32[1,768]{1,0:T(1,128)S(1)}, f32[1,768]{1,0:T(1,128)S(1)}, u32[]{:S(2)}, u32[]{:S(2)}) %collective-permute-start.132) | collective-permute-done | bytes 3104 | tf_op jit(solution)/shard_map/ppermute | solution.py:523
  (1100 shorter events, 245.7 us)
Async XLA Ops:
  3.2 41.7 %collective-permute-start.33 = (bf16[128,768]{1,0:T(8,128)(2,1)S(1)}, bf16[128,768]{1,0:T(8,128)(2,1)S(1)}, u32[]{:S(2)}, u32[]{:S(2)}) collective-permute-start(bf16[128,768]{1,0:T(8,128)(2,1)S(1)} %norm.3.refs_0_.refs_10_), channel_id=1, source_target_pairs={{0,2},{1,3},{2,0},{3,1},{4,6},{5,7},{6,4},{7,5},{8,10},{9,11},{10,... | collective-permute-start | bytes 589832 | tf_op jit(solution)/shard_map/ppermute | solution.py:523
  6.2 39.7 %collective-permute-start.32 = (bf16[128,768]{1,0:T(8,128)(2,1)S(1)}, bf16[128,768]{1,0:T(8,128)(2,1)S(1)}, u32[]{:S(2)}, u32[]{:S(2)}) collective-permute-start(bf16[128,768]{1,0:T(8,128)(2,1)S(1)} %norm.3.refs_0_.refs_10_), channel_id=1, source_target_pairs={{0,1},{1,0},{2,3},{3,2},{4,5},{5,4},{6,7},{7,6},{8,9},{9,8},{10,11... | collective-permute-start | bytes 589832 | tf_op jit(solution)/shard_map/ppermute | solution.py:523
  6.4 29.5 %collective-permute-start.1 = (bf16[128,768]{1,0:T(8,128)(2,1)S(1)}, bf16[128,768]{1,0:T(8,128)(2,1)S(1)}, u32[]{:S(2)}, u32[]{:S(2)}) collective-permute-start(bf16[128,768]{1,0:T(8,128)(2,1)S(1)} %norm.2.refs_0_), channel_id=1, source_target_pairs={{0,2},{1,3},{2,0},{3,1},{4,6},{5,7},{6,4},{7,5},{8,10},{9,11},{10,... | collective-permute-start | bytes 589832 | tf_op jit(solution)/shard_map/ppermute | solution.py:523
  6.6 29.5 %collective-permute-start = (bf16[128,768]{1,0:T(8,128)(2,1)S(1)}, bf16[128,768]{1,0:T(8,128)(2,1)S(1)}, u32[]{:S(2)}, u32[]{:S(2)}) collective-permute-start(bf16[128,768]{1,0:T(8,128)(2,1)S(1)} %norm.2.refs_0_), channel_id=1, source_target_pairs={{0,1},{1,0},{2,3},{3,2},{4,5},{5,4},{6,7},{7,6},{8,9},{9,8},{10,11... | collective-permute-start | bytes 589832 | tf_op jit(solution)/shard_map/ppermute | solution.py:523
  44.8 10.5 %collective-permute-start.3 = (bf16[256,768]{1,0:T(8,128)(2,1)S(1)}, bf16[256,768]{1,0:T(8,128)(2,1)S(1)}, u32[]{:S(2)}, u32[]{:S(2)}) collective-permute-start(bf16[256,768]{1,0:T(8,128)(2,1)S(1)} %get-tuple-element.176), channel_id=1, source_target_pairs={{0,1},{1,0},{2,3},{3,2},{4,5},{5,4},{6,7},{7,6},{8,9},{9,8},{10,11... | collective-permute-start | bytes 1179656 | tf_op jit(solution)/shard_map/ppermute | solution.py:523
  55.1 17.4 %collective-permute-start.35 = (bf16[256,768]{1,0:T(8,128)(2,1)}, bf16[256,768]{1,0:T(8,128)(2,1)S(1)}, u32[]{:S(2)}, u32[]{:S(2)}) collective-permute-start(bf16[256,768]{1,0:T(8,128)(2,1)} %get-tuple-element.209), channel_id=1, source_target_pairs={{0,1},{1,0},{2,3},{3,2},{4,5},{5,4},{6,7},{7,6},{8,9},{9,8},{10,11... | collective-permute-start | bytes 1179656 | tf_op jit(solution)/shard_map/ppermute | solution.py:523
  55.3 7.3 %collective-permute-start.4 = (bf16[128,768]{1,0:T(8,128)(2,1)S(1)}, bf16[128,768]{1,0:T(8,128)(2,1)S(1)}, u32[]{:S(2)}, u32[]{:S(2)}) collective-permute-start(bf16[128,768]{1,0:T(8,128)(2,1)S(1)} %add_far.8), channel_id=1, source_target_pairs={{0,2},{1,3},{2,0},{3,1},{4,6},{5,7},{6,4},{7,5},{8,10},{9,11},{10,... | collective-permute-start | bytes 589832 | tf_op jit(solution)/shard_map/ppermute | solution.py:523
  65.6 9.4 %collective-permute-start.7 = (bf16[48,768]{1,0:T(8,128)(2,1)S(1)}, bf16[48,768]{1,0:T(8,128)(2,1)S(1)}, u32[]{:S(2)}, u32[]{:S(2)}) collective-permute-start(bf16[48,768]{1,0:T(8,128)(2,1)S(1)} %get-tuple-element.179), channel_id=1, source_target_pairs={{0,6},{1,7},{2,4},{3,5},{4,2},{5,3},{6,0},{7,1},{8,14},{9,15},{10,... | collective-permute-start | bytes 221192 | tf_op jit(solution)/shard_map/ppermute | solution.py:538
  68.2 7.3 %collective-permute-start.5 = (bf16[48,768]{1,0:T(8,128)(2,1)S(1)}, bf16[48,768]{1,0:T(8,128)(2,1)S(1)}, u32[]{:S(2)}, u32[]{:S(2)}) collective-permute-start(bf16[48,768]{1,0:T(8,128)(2,1)S(1)} %get-tuple-element.179), channel_id=1, source_target_pairs={{0,4},{4,0},{1,5},{5,1},{2,6},{6,2},{3,7},{7,3},{8,12},{12,8},{9,1... | collective-permute-start | bytes 221192 | tf_op jit(solution)/shard_map/ppermute | solution.py:523
  68.7 6.9 %collective-permute-start.6 = (bf16[48,768]{1,0:T(8,128)(2,1)S(1)}, bf16[48,768]{1,0:T(8,128)(2,1)S(1)}, u32[]{:S(2)}, u32[]{:S(2)}) collective-permute-start(bf16[48,768]{1,0:T(8,128)(2,1)S(1)} %get-tuple-element.178.refs_0_), channel_id=1, source_target_pairs={{0,2},{1,3},{2,0},{3,1},{4,6},{5,7},{6,4},{7,5},{8,10},{9,11},{10,... | collective-permute-start | bytes 221192 | tf_op jit(solution)/shard_map/ppermute | solution.py:523
  73.4 6.8 %collective-permute-start.36 = (bf16[128,768]{1,0:T(8,128)(2,1)}, bf16[128,768]{1,0:T(8,128)(2,1)}, u32[]{:S(2)}, u32[]{:S(2)}) collective-permute-start(bf16[128,768]{1,0:T(8,128)(2,1)} %add_far.10), channel_id=1, source_target_pairs={{0,2},{1,3},{2,0},{3,1},{4,6},{5,7},{6,4},{7,5},{8,10},{9,11},{10,... | collective-permute-start | bytes 589832 | tf_op jit(solution)/shard_map/ppermute | solution.py:523
  79.9 15.1 %collective-permute-start.12 = (bf16[192,768]{1,0:T(8,128)(2,1)}, bf16[192,768]{1,0:T(8,128)(2,1)}, u32[]{:S(2)}, u32[]{:S(2)}) collective-permute-start(bf16[192,768]{1,0:T(8,128)(2,1)} %get-tuple-element.181), channel_id=1, source_target_pairs={{0,1},{1,0},{2,3},{3,2},{4,5},{5,4},{6,7},{7,6},{8,9},{9,8},{10,11... | collective-permute-start | bytes 884744 | tf_op jit(solution)/shard_map/ppermute | solution.py:523
  94.6 11.2 %collective-permute-start.44 = (bf16[192,768]{1,0:T(8,128)(2,1)S(1)}, bf16[192,768]{1,0:T(8,128)(2,1)S(1)}, u32[]{:S(2)}, u32[]{:S(2)}) collective-permute-start(bf16[192,768]{1,0:T(8,128)(2,1)S(1)} %get-tuple-element.214), channel_id=1, source_target_pairs={{0,1},{1,0},{2,3},{3,2},{4,5},{5,4},{6,7},{7,6},{8,9},{9,8},{10,11... | collective-permute-start | bytes 884744 | tf_op jit(solution)/shard_map/ppermute | solution.py:523
  105.1 12.4 %collective-permute-start.17 = (bf16[128,768]{1,0:T(8,128)(2,1)S(1)}, bf16[128,768]{1,0:T(8,128)(2,1)S(1)}, u32[]{:S(2)}, u32[]{:S(2)}) collective-permute-start(bf16[128,768]{1,0:T(8,128)(2,1)S(1)} %get-tuple-element.190.refs_0_), channel_id=1, source_target_pairs={{0,2},{1,3},{2,0},{3,1},{4,6},{5,7},{6,4},{7,5},{8,10},{9,11},{10,... | collective-permute-start | bytes 589832 | tf_op jit(solution)/shard_map/ppermute | solution.py:523
  118.0 12.4 %collective-permute-start.48 = (bf16[128,768]{1,0:T(8,128)(2,1)S(1)}, bf16[128,768]{1,0:T(8,128)(2,1)S(1)}, u32[]{:S(2)}, u32[]{:S(2)}) collective-permute-start(bf16[128,768]{1,0:T(8,128)(2,1)S(1)} %get-tuple-element.223.refs_0_.refs_10_), channel_id=1, source_target_pairs={{0,1},{1,0},{2,3},{3,2},{4,5},{5,4},{6,7},{7,6},{8,9},{9,8},{10,11... | collective-permute-start | bytes 589832 | tf_op jit(solution)/shard_map/ppermute | solution.py:523
  121.6 8.9 %collective-permute-start.50 = (bf16[128,768]{1,0:T(8,128)(2,1)S(1)}, bf16[128,768]{1,0:T(8,128)(2,1)S(1)}, u32[]{:S(2)}, u32[]{:S(2)}) collective-permute-start(bf16[128,768]{1,0:T(8,128)(2,1)S(1)} %collective-permute-done.49.refs_2_.refs_12_), channel_id=1, source_target_pairs={{0,1},{1,0},{2,3},{3,2},{4,5},{5,4},{6,7},{7,6},{8,9},{9,8},{10,11... | collective-permute-start | bytes 589832 | tf_op jit(solution)/shard_map/ppermute | solution.py:523
  129.9 9.1 %collective-permute-start.19 = (bf16[256,768]{1,0:T(8,128)(2,1)S(1)}, bf16[256,768]{1,0:T(8,128)(2,1)S(1)}, u32[]{:S(2)}, u32[]{:S(2)}) collective-permute-start(bf16[256,768]{1,0:T(8,128)(2,1)S(1)} %get-tuple-element.192), channel_id=1, source_target_pairs={{0,1},{1,0},{2,3},{3,2},{4,5},{5,4},{6,7},{7,6},{8,9},{9,8},{10,11... | collective-permute-start | bytes 1179656 | tf_op jit(solution)/shard_map/ppermute | solution.py:523
  139.0 20.0 %collective-permute-start.51 = (bf16[256,768]{1,0:T(8,128)(2,1)}, bf16[256,768]{1,0:T(8,128)(2,1)}, u32[]{:S(2)}, u32[]{:S(2)}) collective-permute-start(bf16[256,768]{1,0:T(8,128)(2,1)} %get-tuple-element.225), channel_id=1, source_target_pairs={{0,1},{1,0},{2,3},{3,2},{4,5},{5,4},{6,7},{7,6},{8,9},{9,8},{10,11... | collective-permute-start | bytes 1179656 | tf_op jit(solution)/shard_map/ppermute | solution.py:523
  139.8 7.7 %collective-permute-start.20 = (bf16[128,768]{1,0:T(8,128)(2,1)}, bf16[128,768]{1,0:T(8,128)(2,1)}, u32[]{:S(2)}, u32[]{:S(2)}) collective-permute-start(bf16[128,768]{1,0:T(8,128)(2,1)} %add_far.9), channel_id=1, source_target_pairs={{0,2},{1,3},{2,0},{3,1},{4,6},{5,7},{6,4},{7,5},{8,10},{9,11},{10,... | collective-permute-start | bytes 589832 | tf_op jit(solution)/shard_map/ppermute | solution.py:523
  155.5 7.2 %collective-permute-start.23 = (bf16[48,768]{1,0:T(8,128)(2,1)S(1)}, bf16[48,768]{1,0:T(8,128)(2,1)S(1)}, u32[]{:S(2)}, u32[]{:S(2)}) collective-permute-start(bf16[48,768]{1,0:T(8,128)(2,1)S(1)} %get-tuple-element.197), channel_id=1, source_target_pairs={{0,6},{1,7},{2,4},{3,5},{4,2},{5,3},{6,0},{7,1},{8,14},{9,15},{10,... | collective-permute-start | bytes 221192 | tf_op jit(solution)/shard_map/ppermute | solution.py:538
  161.0 8.1 %collective-permute-start.52 = (bf16[128,768]{1,0:T(8,128)(2,1)S(1)}, bf16[128,768]{1,0:T(8,128)(2,1)S(1)}, u32[]{:S(2)}, u32[]{:S(2)}) collective-permute-start(bf16[128,768]{1,0:T(8,128)(2,1)S(1)} %add_far.11), channel_id=1, source_target_pairs={{0,2},{1,3},{2,0},{3,1},{4,6},{5,7},{6,4},{7,5},{8,10},{9,11},{10,... | collective-permute-start | bytes 589832 | tf_op jit(solution)/shard_map/ppermute | solution.py:523
  167.4 22.0 %collective-permute-start.28 = (bf16[192,768]{1,0:T(8,128)(2,1)}, bf16[192,768]{1,0:T(8,128)(2,1)}, u32[]{:S(2)}, u32[]{:S(2)}) collective-permute-start(bf16[192,768]{1,0:T(8,128)(2,1)} %get-tuple-element.199), channel_id=1, source_target_pairs={{0,1},{1,0},{2,3},{3,2},{4,5},{5,4},{6,7},{7,6},{8,9},{9,8},{10,11... | collective-permute-start | bytes 884744 | tf_op jit(solution)/shard_map/ppermute | solution.py:523
  191.2 6.7 %collective-permute-start.30 = (bf16[48,768]{1,0:T(8,128)(2,1)S(1)}, bf16[48,768]{1,0:T(8,128)(2,1)S(1)}, u32[]{:S(2)}, u32[]{:S(2)}) collective-permute-start(bf16[48,768]{1,0:T(8,128)(2,1)S(1)} %get-tuple-element.202), channel_id=1, source_target_pairs={{0,2},{1,3},{2,0},{3,1},{4,6},{5,7},{6,4},{7,5},{8,10},{9,11},{10,... | collective-permute-start | bytes 221192 | tf_op jit(solution)/shard_map/ppermute | solution.py:523
  194.3 9.4 %collective-permute-start.61 = (bf16[48,768]{1,0:T(8,128)(2,1)S(1)}, bf16[48,768]{1,0:T(8,128)(2,1)S(1)}, u32[]{:S(2)}, u32[]{:S(2)}) collective-permute-start(bf16[48,768]{1,0:T(8,128)(2,1)S(1)} %get-tuple-element.234), channel_id=1, source_target_pairs={{0,4},{4,0},{1,5},{5,1},{2,6},{6,2},{3,7},{7,3},{8,12},{12,8},{9,1... | collective-permute-start | bytes 221192 | tf_op jit(solution)/shard_map/ppermute | solution.py:523
  194.9 8.8 %collective-permute-start.62 = (bf16[48,768]{1,0:T(8,128)(2,1)S(1)}, bf16[48,768]{1,0:T(8,128)(2,1)S(1)}, u32[]{:S(2)}, u32[]{:S(2)}) collective-permute-start(bf16[48,768]{1,0:T(8,128)(2,1)S(1)} %get-tuple-element.235), channel_id=1, source_target_pairs={{0,2},{1,3},{2,0},{3,1},{4,6},{5,7},{6,4},{7,5},{8,10},{9,11},{10,... | collective-permute-start | bytes 221192 | tf_op jit(solution)/shard_map/ppermute | solution.py:523
  196.4 9.0 %collective-permute-start.63 = (bf16[48,768]{1,0:T(8,128)(2,1)S(1)}, bf16[48,768]{1,0:T(8,128)(2,1)S(1)}, u32[]{:S(2)}, u32[]{:S(2)}) collective-permute-start(bf16[48,768]{1,0:T(8,128)(2,1)S(1)} %get-tuple-element.236), channel_id=1, source_target_pairs={{0,6},{1,7},{2,4},{3,5},{4,2},{5,3},{6,0},{7,1},{8,14},{9,15},{10,... | collective-permute-start | bytes 221192 | tf_op jit(solution)/shard_map/ppermute | solution.py:538
  201.8 8.4 %collective-permute-start.66 = (bf16[48,768]{1,0:T(8,128)(2,1)S(1)}, bf16[48,768]{1,0:T(8,128)(2,1)S(1)}, u32[]{:S(2)}, u32[]{:S(2)}) collective-permute-start(bf16[48,768]{1,0:T(8,128)(2,1)S(1)} %get-tuple-element.242), channel_id=1, source_target_pairs={{0,6},{1,7},{2,4},{3,5},{4,2},{5,3},{6,0},{7,1},{8,14},{9,15},{10,... | collective-permute-start | bytes 221192 | tf_op jit(solution)/shard_map/ppermute | solution.py:538
  203.2 7.5 %collective-permute-start.64 = (bf16[48,768]{1,0:T(8,128)(2,1)S(1)}, bf16[48,768]{1,0:T(8,128)(2,1)S(1)}, u32[]{:S(2)}, u32[]{:S(2)}) collective-permute-start(bf16[48,768]{1,0:T(8,128)(2,1)S(1)} %get-tuple-element.242), channel_id=1, source_target_pairs={{0,4},{4,0},{1,5},{5,1},{2,6},{6,2},{3,7},{7,3},{8,12},{12,8},{9,1... | collective-permute-start | bytes 221192 | tf_op jit(solution)/shard_map/ppermute | solution.py:523
  203.7 8.7 %collective-permute-start.67 = (bf16[48,768]{1,0:T(8,128)(2,1)S(1)}, bf16[48,768]{1,0:T(8,128)(2,1)S(1)}, u32[]{:S(2)}, u32[]{:S(2)}) collective-permute-start(bf16[48,768]{1,0:T(8,128)(2,1)S(1)} %get-tuple-element.241.refs_8_), channel_id=1, source_target_pairs={{0,1},{1,0},{2,3},{3,2},{4,5},{5,4},{6,7},{7,6},{8,9},{9,8},{10,11... | collective-permute-start | bytes 221192 | tf_op jit(solution)/shard_map/ppermute | solution.py:523
  203.7 8.6 %collective-permute-start.65 = (bf16[48,768]{1,0:T(8,128)(2,1)S(1)}, bf16[48,768]{1,0:T(8,128)(2,1)S(1)}, u32[]{:S(2)}, u32[]{:S(2)}) collective-permute-start(bf16[48,768]{1,0:T(8,128)(2,1)S(1)} %get-tuple-element.241.refs_8_), channel_id=1, source_target_pairs={{0,2},{1,3},{2,0},{3,1},{4,6},{5,7},{6,4},{7,5},{8,10},{9,11},{10,... | collective-permute-start | bytes 221192 | tf_op jit(solution)/shard_map/ppermute | solution.py:523
  236.5 17.8 %collective-permute-start.76 = (bf16[128,768]{1,0:T(8,128)(2,1)}, bf16[128,768]{1,0:T(8,128)(2,1)}, u32[]{:S(2)}, u32[]{:S(2)}) collective-permute-start(bf16[128,768]{1,0:T(8,128)(2,1)} %get-tuple-element.250.refs_0_.refs_4_), channel_id=1, source_target_pairs={{0,2},{1,3},{2,0},{3,1},{4,6},{5,7},{6,4},{7,5},{8,10},{9,11},{10,... | collective-permute-start | bytes 589832 | tf_op jit(solution)/shard_map/ppermute | solution.py:523
  237.2 21.3 %collective-permute-start.108 = (bf16[128,768]{1,0:T(8,128)(2,1)}, bf16[128,768]{1,0:T(8,128)(2,1)}, u32[]{:S(2)}, u32[]{:S(2)}) collective-permute-start(bf16[128,768]{1,0:T(8,128)(2,1)} %get-tuple-element.285.refs_0_.refs_14_), channel_id=1, source_target_pairs={{0,2},{1,3},{2,0},{3,1},{4,6},{5,7},{6,4},{7,5},{8,10},{9,11},{10,... | collective-permute-start | bytes 589832 | tf_op jit(solution)/shard_map/ppermute | solution.py:523
  239.2 12.7 %collective-permute-start.144 = (f32[13,768]{1,0:T(8,128)}, f32[13,768]{1,0:T(8,128)}, u32[]{:S(2)}, u32[]{:S(2)}) collective-permute-start(f32[13,768]{1,0:T(8,128)} %fusion.32), channel_id=1, source_target_pairs={{0,2},{1,3},{2,0},{3,1},{4,6},{5,7},{6,4},{7,5},{8,10},{9,11},{10,... | collective-permute-start | bytes 119816 | tf_op jit(solution)/shard_map/ppermute | solution.py:523
  251.9 27.6 %collective-permute-start.75 = (bf16[128,768]{1,0:T(8,128)(2,1)}, bf16[128,768]{1,0:T(8,128)(2,1)S(1)}, u32[]{:S(2)}, u32[]{:S(2)}) collective-permute-start(bf16[128,768]{1,0:T(8,128)(2,1)} %get-tuple-element.250.refs_0_.refs_4_), channel_id=1, source_target_pairs={{0,1},{1,0},{2,3},{3,2},{4,5},{5,4},{6,7},{7,6},{8,9},{9,8},{10,11... | collective-permute-start | bytes 589832 | tf_op jit(solution)/shard_map/ppermute | solution.py:523
  254.3 25.2 %collective-permute-start.77 = (bf16[128,768]{1,0:T(8,128)(2,1)}, bf16[128,768]{1,0:T(8,128)(2,1)S(1)}, u32[]{:S(2)}, u32[]{:S(2)}) collective-permute-start(bf16[128,768]{1,0:T(8,128)(2,1)} %collective-permute-done.76.refs_2_.refs_6_), channel_id=1, source_target_pairs={{0,1},{1,0},{2,3},{3,2},{4,5},{5,4},{6,7},{7,6},{8,9},{9,8},{10,11... | collective-permute-start | bytes 589832 | tf_op jit(solution)/shard_map/ppermute | solution.py:523
  255.3 34.3 %collective-permute-start.107 = (bf16[128,768]{1,0:T(8,128)(2,1)}, bf16[128,768]{1,0:T(8,128)(2,1)S(1)}, u32[]{:S(2)}, u32[]{:S(2)}) collective-permute-start(bf16[128,768]{1,0:T(8,128)(2,1)} %get-tuple-element.285.refs_0_.refs_14_), channel_id=1, source_target_pairs={{0,1},{1,0},{2,3},{3,2},{4,5},{5,4},{6,7},{7,6},{8,9},{9,8},{10,11... | collective-permute-start | bytes 589832 | tf_op jit(solution)/shard_map/ppermute | solution.py:523
  256.9 19.8 %collective-permute-start.146 = (f32[13,768]{1,0:T(8,128)S(1)}, f32[13,768]{1,0:T(8,128)S(1)}, u32[]{:S(2)}, u32[]{:S(2)}) collective-permute-start(f32[13,768]{1,0:T(8,128)S(1)} %add.219), channel_id=1, source_target_pairs={{0,8},{8,0},{16,24},{24,16},{1,9},{9,1},{17,25},{25,17},{2,10},{10... | collective-permute-start | bytes 119816 | tf_op jit(solution)/shard_map/ppermute | solution.py:523
  258.5 31.0 %collective-permute-start.109 = (bf16[128,768]{1,0:T(8,128)(2,1)}, bf16[128,768]{1,0:T(8,128)(2,1)S(1)}, u32[]{:S(2)}, u32[]{:S(2)}) collective-permute-start(bf16[128,768]{1,0:T(8,128)(2,1)} %collective-permute-done.108.refs_2_.refs_16_), channel_id=1, source_target_pairs={{0,1},{1,0},{2,3},{3,2},{4,5},{5,4},{6,7},{7,6},{8,9},{9,8},{10,11... | collective-permute-start | bytes 589832 | tf_op jit(solution)/shard_map/ppermute | solution.py:523
  276.7 22.6 %collective-permute-start.147 = (f32[13,768]{1,0:T(8,128)S(1)}, f32[13,768]{1,0:T(8,128)S(1)}, u32[]{:S(2)}, u32[]{:S(2)}) collective-permute-start(f32[13,768]{1,0:T(8,128)S(1)} %add.220), channel_id=1, source_target_pairs={{0,16},{8,24},{16,0},{24,8},{1,17},{9,25},{17,1},{25,9},{2,18},{10... | collective-permute-start | bytes 119816 | tf_op jit(solution)/shard_map/ppermute | solution.py:523
  289.2 11.8 %collective-permute-start.78 = (bf16[256,768]{1,0:T(8,128)(2,1)S(1)}, bf16[256,768]{1,0:T(8,128)(2,1)S(1)}, u32[]{:S(2)}, u32[]{:S(2)}) collective-permute-start(bf16[256,768]{1,0:T(8,128)(2,1)S(1)} %get-tuple-element.254), channel_id=1, source_target_pairs={{0,1},{1,0},{2,3},{3,2},{4,5},{5,4},{6,7},{7,6},{8,9},{9,8},{10,11... | collective-permute-start | bytes 1179656 | tf_op jit(solution)/shard_map/ppermute | solution.py:523
  297.5 27.6 %collective-permute-start.159 = (bf16[192,1536]{1,0:T(8,128)(2,1)S(1)}, bf16[192,1536]{1,0:T(8,128)(2,1)S(1)}, u32[]{:S(2)}, u32[]{:S(2)}) collective-permute-start(bf16[192,1536]{1,0:T(8,128)(2,1)S(1)} %get-tuple-element.377), channel_id=1, source_target_pairs={{0,8},{8,0},{16,24},{24,16},{1,9},{9,1},{17,25},{25,17},{2,10},{10... | collective-permute-start | bytes 1769480 | tf_op jit(solution)/shard_map/ppermute | solution.py:523
  298.0 28.2 %collective-permute-start.161 = (bf16[192,1536]{1,0:T(8,128)(2,1)S(1)}, bf16[192,1536]{1,0:T(8,128)(2,1)S(1)}, u32[]{:S(2)}, u32[]{:S(2)}) collective-permute-start(bf16[192,1536]{1,0:T(8,128)(2,1)S(1)} %get-tuple-element.378), channel_id=1, source_target_pairs={{0,24},{8,16},{16,8},{24,0},{1,25},{9,17},{17,9},{25,1},{2,26},{10... | collective-permute-start | bytes 1769480 | tf_op jit(solution)/shard_map/ppermute | solution.py:523
  299.3 52.8 %collective-permute-start.160 = (bf16[192,1536]{1,0:T(8,128)(2,1)S(1)}, bf16[192,1536]{1,0:T(8,128)(2,1)S(1)}, u32[]{:S(2)}, u32[]{:S(2)}) collective-permute-start(bf16[192,1536]{1,0:T(8,128)(2,1)S(1)} %get-tuple-element.379), channel_id=1, source_target_pairs={{0,16},{8,24},{16,0},{24,8},{1,17},{9,25},{17,1},{25,9},{2,18},{10... | collective-permute-start | bytes 1769480 | tf_op jit(solution)/shard_map/ppermute | solution.py:523
  301.1 7.9 %collective-permute-start.79 = (bf16[128,768]{1,0:T(8,128)(2,1)S(1)}, bf16[128,768]{1,0:T(8,128)(2,1)S(1)}, u32[]{:S(2)}, u32[]{:S(2)}) collective-permute-start(bf16[128,768]{1,0:T(8,128)(2,1)S(1)} %add_far.12), channel_id=1, source_target_pairs={{0,2},{1,3},{2,0},{3,1},{4,6},{5,7},{6,4},{7,5},{8,10},{9,11},{10,... | collective-permute-start | bytes 589832 | tf_op jit(solution)/shard_map/ppermute | solution.py:523
  302.7 10.7 %collective-permute-start.111 = (bf16[128,768]{1,0:T(8,128)(2,1)S(1)}, bf16[128,768]{1,0:T(8,128)(2,1)S(1)}, u32[]{:S(2)}, u32[]{:S(2)}) collective-permute-start(bf16[128,768]{1,0:T(8,128)(2,1)S(1)} %add_far.14), channel_id=1, source_target_pairs={{0,2},{1,3},{2,0},{3,1},{4,6},{5,7},{6,4},{7,5},{8,10},{9,11},{10,... | collective-permute-start | bytes 589832 | tf_op jit(solution)/shard_map/ppermute | solution.py:523
  309.0 44.9 %collective-permute-start.152 = (bf16[4,96,768]{2,1,0:T(8,128)(2,1)S(1)}, bf16[4,96,768]{2,1,0:T(8,128)(2,1)S(1)}, u32[]{:S(2)}, u32[]{:S(2)}) collective-permute-start(bf16[4,96,768]{2,1,0:T(8,128)(2,1)S(1)} %dynamic-slice_bitcast_fusion.6), channel_id=1, source_target_pairs={{0,4},{4,0},{1,5},{5,1},{2,6},{6,2},{3,7},{7,3},{8,12},{12,8},{9,1... | collective-permute-start | bytes 1769480 | tf_op jit(solution)/shard_map/ppermute | solution.py:523
  316.1 36.2 %collective-permute-start.133 = (f32[1,768]{1,0:T(1,128)S(1)}, f32[1,768]{1,0:T(1,128)S(1)}, u32[]{:S(2)}, u32[]{:S(2)}) collective-permute-start(f32[1,768]{1,0:T(1,128)S(1)} %slice_add_fusion.2), channel_id=1, source_target_pairs={{0,1},{1,0},{2,3},{3,2},{4,5},{5,4},{6,7},{7,6},{8,9},{9,8},{10,11... | collective-permute-start | bytes 9224 | tf_op jit(solution)/shard_map/ppermute | solution.py:523
  357.5 14.9 %collective-permute-start.153 = (bf16[96,768]{1,0:T(8,128)(2,1)S(1)}, bf16[96,768]{1,0:T(8,128)(2,1)S(1)}, u32[]{:S(2)}, u32[]{:S(2)}) collective-permute-start(bf16[96,768]{1,0:T(8,128)(2,1)S(1)} %get-tuple-element.405), channel_id=1, source_target_pairs={{0,8},{8,0},{16,24},{24,16},{1,9},{9,1},{17,25},{25,17},{2,10},{10... | collective-permute-start | bytes 442376 | tf_op jit(solution)/shard_map/ppermute | solution.py:523
  357.6 14.9 %collective-permute-start.155 = (bf16[96,768]{1,0:T(8,128)(2,1)S(1)}, bf16[96,768]{1,0:T(8,128)(2,1)S(1)}, u32[]{:S(2)}, u32[]{:S(2)}) collective-permute-start(bf16[96,768]{1,0:T(8,128)(2,1)S(1)} %get-tuple-element.406), channel_id=1, source_target_pairs={{0,24},{8,16},{16,8},{24,0},{1,25},{9,17},{17,9},{25,1},{2,26},{10... | collective-permute-start | bytes 442376 | tf_op jit(solution)/shard_map/ppermute | solution.py:523
  358.8 15.1 %collective-permute-start.154 = (bf16[96,768]{1,0:T(8,128)(2,1)S(1)}, bf16[96,768]{1,0:T(8,128)(2,1)S(1)}, u32[]{:S(2)}, u32[]{:S(2)}) collective-permute-start(bf16[96,768]{1,0:T(8,128)(2,1)S(1)} %get-tuple-element.407), channel_id=1, source_target_pairs={{0,16},{8,24},{16,0},{24,8},{1,17},{9,25},{17,1},{25,9},{2,18},{10... | collective-permute-start | bytes 442376 | tf_op jit(solution)/shard_map/ppermute | solution.py:523
  368.4 7.1 %collective-permute-start.82 = (bf16[48,768]{1,0:T(8,128)(2,1)S(1)}, bf16[48,768]{1,0:T(8,128)(2,1)S(1)}, u32[]{:S(2)}, u32[]{:S(2)}) collective-permute-start(bf16[48,768]{1,0:T(8,128)(2,1)S(1)} %get-tuple-element.259), channel_id=1, source_target_pairs={{0,6},{1,7},{2,4},{3,5},{4,2},{5,3},{6,0},{7,1},{8,14},{9,15},{10,... | collective-permute-start | bytes 221192 | tf_op jit(solution)/shard_map/ppermute | solution.py:538
  413.6 31.3 %collective-permute-start.156 = (bf16[192,1536]{1,0:T(8,128)(2,1)S(1)}, bf16[192,1536]{1,0:T(8,128)(2,1)S(1)}, u32[]{:S(2)}, u32[]{:S(2)}) collective-permute-start(bf16[192,1536]{1,0:T(8,128)(2,1)S(1)} %get-tuple-element.374), channel_id=1, source_target_pairs={{0,8},{8,0},{16,24},{24,16},{1,9},{9,1},{17,25},{25,17},{2,10},{10... | collective-permute-start | bytes 1769480 | tf_op jit(solution)/shard_map/ppermute | solution.py:523
  415.2 29.7 %collective-permute-start.158 = (bf16[192,1536]{1,0:T(8,128)(2,1)S(1)}, bf16[192,1536]{1,0:T(8,128)(2,1)S(1)}, u32[]{:S(2)}, u32[]{:S(2)}) collective-permute-start(bf16[192,1536]{1,0:T(8,128)(2,1)S(1)} %get-tuple-element.375), channel_id=1, source_target_pairs={{0,24},{8,16},{16,8},{24,0},{1,25},{9,17},{17,9},{25,1},{2,26},{10... | collective-permute-start | bytes 1769480 | tf_op jit(solution)/shard_map/ppermute | solution.py:523
  417.5 48.4 %collective-permute-start.157 = (bf16[192,1536]{1,0:T(8,128)(2,1)S(1)}, bf16[192,1536]{1,0:T(8,128)(2,1)S(1)}, u32[]{:S(2)}, u32[]{:S(2)}) collective-permute-start(bf16[192,1536]{1,0:T(8,128)(2,1)S(1)} %get-tuple-element.376), channel_id=1, source_target_pairs={{0,16},{8,24},{16,0},{24,8},{1,17},{9,25},{17,1},{25,9},{2,18},{10... | collective-permute-start | bytes 1769480 | tf_op jit(solution)/shard_map/ppermute | solution.py:523
  429.8 8.1 %collective-permute-start.123 = (bf16[128,768]{1,0:T(8,128)(2,1)S(1)}, bf16[128,768]{1,0:T(8,128)(2,1)S(1)}, u32[]{:S(2)}, u32[]{:S(2)}) collective-permute-start(bf16[128,768]{1,0:T(8,128)(2,1)S(1)} %get-tuple-element.303.refs_0_.refs_14_), channel_id=1, source_target_pairs={{0,1},{1,0},{2,3},{3,2},{4,5},{5,4},{6,7},{7,6},{8,9},{9,8},{10,11... | collective-permute-start | bytes 589832 | tf_op jit(solution)/shard_map/ppermute | solution.py:523
  429.8 8.2 %collective-permute-start.125 = (bf16[128,768]{1,0:T(8,128)(2,1)S(1)}, bf16[128,768]{1,0:T(8,128)(2,1)S(1)}, u32[]{:S(2)}, u32[]{:S(2)}) collective-permute-start(bf16[128,768]{1,0:T(8,128)(2,1)S(1)} %collective-permute-done.124.refs_2_.refs_16_), channel_id=1, source_target_pairs={{0,1},{1,0},{2,3},{3,2},{4,5},{5,4},{6,7},{7,6},{8,9},{9,8},{10,11... | collective-permute-start | bytes 589832 | tf_op jit(solution)/shard_map/ppermute | solution.py:523
  437.9 32.0 %collective-permute-start.94 = (bf16[256,768]{1,0:T(8,128)(2,1)S(1)}, bf16[256,768]{1,0:T(8,128)(2,1)S(1)}, u32[]{:S(2)}, u32[]{:S(2)}) collective-permute-start(bf16[256,768]{1,0:T(8,128)(2,1)S(1)} %get-tuple-element.272), channel_id=1, source_target_pairs={{0,1},{1,0},{2,3},{3,2},{4,5},{5,4},{6,7},{7,6},{8,9},{9,8},{10,11... | collective-permute-start | bytes 1179656 | tf_op jit(solution)/shard_map/ppermute | solution.py:523
  444.3 26.3 %collective-permute-start.126 = (bf16[256,768]{1,0:T(8,128)(2,1)S(1)}, bf16[256,768]{1,0:T(8,128)(2,1)S(1)}, u32[]{:S(2)}, u32[]{:S(2)}) collective-permute-start(bf16[256,768]{1,0:T(8,128)(2,1)S(1)} %get-tuple-element.307), channel_id=1, source_target_pairs={{0,1},{1,0},{2,3},{3,2},{4,5},{5,4},{6,7},{7,6},{8,9},{9,8},{10,11... | collective-permute-start | bytes 1179656 | tf_op jit(solution)/shard_map/ppermute | solution.py:523
  470.7 7.1 %collective-permute-start.127 = (bf16[128,768]{1,0:T(8,128)(2,1)S(1)}, bf16[128,768]{1,0:T(8,128)(2,1)S(1)}, u32[]{:S(2)}, u32[]{:S(2)}) collective-permute-start(bf16[128,768]{1,0:T(8,128)(2,1)S(1)} %add_far.15), channel_id=1, source_target_pairs={{0,2},{1,3},{2,0},{3,1},{4,6},{5,7},{6,4},{7,5},{8,10},{9,11},{10,... | collective-permute-start | bytes 589832 | tf_op jit(solution)/shard_map/ppermute | solution.py:523
  472.2 11.5 %collective-permute-start.148 = (bf16[4,96,768]{2,1,0:T(8,128)(2,1)S(1)}, bf16[4,96,768]{2,1,0:T(8,128)(2,1)S(1)}, u32[]{:S(2)}, u32[]{:S(2)}) collective-permute-start(bf16[4,96,768]{2,1,0:T(8,128)(2,1)S(1)} %dynamic-slice_bitcast_fusion.7), channel_id=1, source_target_pairs={{0,4},{4,0},{1,5},{5,1},{2,6},{6,2},{3,7},{7,3},{8,12},{12,8},{9,1... | collective-permute-start | bytes 1769480 | tf_op jit(solution)/shard_map/ppermute | solution.py:523
  486.7 16.6 %collective-permute-start.149 = (bf16[96,768]{1,0:T(8,128)(2,1)S(1)}, bf16[96,768]{1,0:T(8,128)(2,1)S(1)}, u32[]{:S(2)}, u32[]{:S(2)}) collective-permute-start(bf16[96,768]{1,0:T(8,128)(2,1)S(1)} %get-tuple-element.402), channel_id=1, source_target_pairs={{0,8},{8,0},{16,24},{24,16},{1,9},{9,1},{17,25},{25,17},{2,10},{10... | collective-permute-start | bytes 442376 | tf_op jit(solution)/shard_map/ppermute | solution.py:523
  488.8 14.5 %collective-permute-start.151 = (bf16[96,768]{1,0:T(8,128)(2,1)S(1)}, bf16[96,768]{1,0:T(8,128)(2,1)S(1)}, u32[]{:S(2)}, u32[]{:S(2)}) collective-permute-start(bf16[96,768]{1,0:T(8,128)(2,1)S(1)} %get-tuple-element.403), channel_id=1, source_target_pairs={{0,24},{8,16},{16,8},{24,0},{1,25},{9,17},{17,9},{25,1},{2,26},{10... | collective-permute-start | bytes 442376 | tf_op jit(solution)/shard_map/ppermute | solution.py:523
  491.1 12.2 %collective-permute-start.150 = (bf16[96,768]{1,0:T(8,128)(2,1)S(1)}, bf16[96,768]{1,0:T(8,128)(2,1)S(1)}, u32[]{:S(2)}, u32[]{:S(2)}) collective-permute-start(bf16[96,768]{1,0:T(8,128)(2,1)S(1)} %get-tuple-element.404), channel_id=1, source_target_pairs={{0,16},{8,24},{16,0},{24,8},{1,17},{9,25},{17,1},{25,9},{2,18},{10... | collective-permute-start | bytes 442376 | tf_op jit(solution)/shard_map/ppermute | solution.py:523
  491.1 11.6 %collective-permute-start.132 = (f32[1,768]{1,0:T(1,128)S(1)}, f32[1,768]{1,0:T(1,128)S(1)}, u32[]{:S(2)}, u32[]{:S(2)}) collective-permute-start(f32[1,768]{1,0:T(1,128)S(1)} %add.200), channel_id=1, source_target_pairs={{0,16},{8,24},{16,0},{24,8},{1,17},{9,25},{17,1},{25,9},{2,18},{10... | collective-permute-start | bytes 9224 | tf_op jit(solution)/shard_map/ppermute | solution.py:523
  (429 other events, 3155.4 us)
